TPU v7x, 32 devices: a whole 2x2x4 slice. The times are simulated.
32 devices in a mesh: gx: 8 (over z, core), gy: 4 (over y, x).
Axes of the slice: x: 2, y: 2, z: 4, core: 2. Of those that a mesh axis runs over, the one named last changes fastest.
Arguments:
- feature: bfloat16 [6, 64, 192, 512], P(None, None, 'gx', 'gy'), may hold values from -6 to 6
- widths: int32 [8], replicated, may hold values from 8 to 24, as said below
- dw_weight: float32 [27, 64], replicated, may hold values from -1.25 to 1.25
- dw_bias: float32 [64], replicated, may hold values from -3 to 3
- pw_weight: bfloat16 [64, 64], replicated, may hold values from -0.75 to 0.75
- pw_bias: float32 [64], replicated, may hold values from -3 to 3
- lift_weight: float32 [64, 3], replicated, may hold values from -3 to 3
- coarse: float32 [3, 8, 32], P(None, 'gy'), may hold values from -6 to 6
Outputs:
- block_out: bfloat16 [2, 64, 192, 512], P(None, None, 'gx', 'gy')
Inputs may be any that keep to these rules, and one draw needn't show every extreme that they name: The widths sum to 128; some slab has width exactly 24 and some exactly 8.
All inputs are finite; a program needn't handle non-finite values.
Results may differ from a plain program's by a relative error of at most 0.0031.
Values may be sent and summed in bfloat16 or wider, within the bound.
No kernel may reach another device: no remote copies, remote signals or barrier semaphores. Data moves between devices by JAX's collectives and lax.ppermute only.
A program may use at most 64 MiB of HBM per device.

v0:
```python
import functools

import jax
import jax.numpy as jnp
from jax import lax
from jax.experimental import pallas as pl
from jax.experimental.pallas import tpu as pltpu
from jax.sharding import PartitionSpec as P

XW = 16
ZOUT = 2
CF = 16
ROWS = 8
CHUNK = 16
DW_BIAS, PW_BIAS, LIFT = 27, 28, 29
F32 = jnp.float32
BF16 = jnp.bfloat16
VMEM_BYTES = 14 * 1024 * 1024


def lane_iota(shape):
    return lax.broadcasted_iota(jnp.int32, shape, len(shape) - 1)


def row_iota(shape):
    return lax.broadcasted_iota(jnp.int32, shape, len(shape) - 2)


def tap_of(m, dx, dy):
    return 9 * m + 3 * (dx + 1) + (dy + 1)


def is_even(axis):
    return lax.rem(lax.axis_index(axis), 2) == 0


def pack_kernel(
    feature, widths_in, taps_in, dw_bias_in, pw_bias_in, lift_in, coarse_in,
    cells, weights, first, second, own_block, widths,
    planes, widths_here, taps, dw_bias, pw_bias, lift, coarse, stacked, tail, picked, sems, small_sems,
):
    count, channels, slots, tile = feature.shape

    half_of = channels // 2

    def copy_of(m, part):
        at = (pl.ds(ZOUT * m, ZOUT), pl.ds(part * half_of, half_of))
        return pltpu.make_async_copy(feature.at[at], planes.at[at], sems.at[m, part])

    small = [
        pltpu.make_async_copy(source, target, small_sems.at[i])
        for i, (source, target) in enumerate(
            (
                (widths_in, widths_here),
                (taps_in, taps),
                (dw_bias_in, dw_bias),
                (pw_bias_in, pw_bias),
                (lift_in, lift),
                (coarse_in, coarse),
            )
        )
    ]
    for copy in small:
        copy.start()
    for m in range(3):
        for part in range(2):
            copy_of(m, part).start()
    def take_small():
        for copy in small:
            copy.wait()
        for d in range(widths.shape[0]):
            widths[d] = widths_here[d]
        stacked[0:DW_BIAS, :] = taps[...]
        stacked[DW_BIAS : DW_BIAS + 1, :] = dw_bias[...]
        stacked[PW_BIAS : PW_BIAS + 1, :] = pw_bias[...]
        stacked[LIFT : LIFT + 3, :] = lift[...]
        turned = jnp.transpose(stacked[...])
        for t in range(stacked.shape[0]):
            weights[t] = jnp.broadcast_to(turned[:, t : t + 1], (channels, tile))

        own_block[...] = coarse[...]
        parts, own_rows, ncy = coarse.shape
        tail[...] = jnp.zeros_like(tail)
        if 3 * ncy <= tile:
            for k in range(parts):
                rest = coarse[k]
                for p in range(3):
                    term = rest.astype(BF16).astype(F32)
                    rest = rest - term
                    tail[k * own_rows : (k + 1) * own_rows, p * ncy : (p + 1) * ncy] = term
        for message in (first, second):
            message[channels:, :] = tail[...].astype(BF16)

    lane, row = lane_iota((slots, tile)), row_iota((slots, tile))
    mine = (lane >> 3) == (row & 15)
    in_even, in_odd = mine & ((lane & 4) == 0), mine & ((lane & 4) != 0)
    sublane = row_iota((ROWS, tile))

    def placed(m, k):
        both = []
        for z in range(ZOUT):
            plane = planes[ZOUT * m + z, k].astype(F32)
            cells[ZOUT * m + z, k * slots : (k + 1) * slots, :] = plane
            both.append(
                jnp.concatenate(
                    [
                        pltpu.roll(plane[x : x + ROWS], (2 + 4 * z + 8 * x) % tile, 1, stride=8, stride_axis=0)
                        for x in range(0, slots, ROWS)
                    ],
                    axis=0,
                )
            )
        rows = jnp.where(in_even, both[0], jnp.where(in_odd, both[1], 0.0))
        return rows[0:ROWS] + rows[ROWS : 2 * ROWS], rows[2 * ROWS :]

    def summed(m, k, step):
        if step == 0:
            return placed(m, k)
        one, two = summed(m, k, step // 2), summed(m, k + step, step // 2)
        turn = (sublane & step) != 0
        return tuple(
            jnp.where(turn, b, a) + pltpu.roll(jnp.where(turn, a, b), step, 0) for a, b in zip(one, two)
        )

    for m in range(3):
        for part in range(2):
            copy_of(m, part).wait()
            for c in range(part * half_of, (part + 1) * half_of, ROWS):
                for half, total in enumerate(summed(m, c, ROWS // 2)):
                    picked[m, half, c : c + ROWS, :] = total
        if m == 0:
            take_small()
    width = widths_here[lax.axis_index("gx")]

    shape = (channels, tile)
    lane = lane_iota(shape)
    on_left = (lane & 2) != 0
    packed = [None, None]
    for m in range(3):
        low, high = (jnp.where(16 * half + (lane >> 3) < width, picked[m, half], 0.0) for half in range(2))
        moved = {
            -1: tuple(
                pltpu.roll(jnp.where(lane < tile - 16, one, two), 16, 1) for one, two in ((low, high), (high, low))
            ),
            0: (low, high),
            1: tuple(
                pltpu.roll(jnp.where(lane >= 16, one, two), tile - 16, 1) for one, two in ((low, high), (high, low))
            ),
        }
        for dx in (-1, 0, 1):
            weight = jnp.where(on_left, weights[tap_of(m, dx, 1)], weights[tap_of(m, dx, -1)])
            for half in range(2):
                term = weight * moved[dx][half]
                packed[half] = term if packed[half] is None else packed[half] + term
    left = jnp.where(on_left, packed[0], pltpu.roll(packed[1], tile - 2, 1))
    right = jnp.where(on_left, pltpu.roll(packed[1], 2, 1), packed[0])
    first[0:channels, :] = right.astype(BF16)
    second[0:channels, :] = left.astype(BF16)


def shifted_sum(before, centre, after):
    lane = lane_iota(centre.shape)
    tile = centre.shape[-1]
    before = jnp.where(lane < 2, 0.0, pltpu.roll(before, 2, 1))
    after = jnp.where(lane >= tile - 2, 0.0, pltpu.roll(after, tile - 2, 1))
    return centre + before + after


def convolve_block(cells, weights, depth, b, limit):
    channels = weights.shape[1]
    slots = cells.shape[1] // channels
    at = pl.ds(pl.multiple_of(b * ROWS, ROWS), ROWS)
    tap = [weights[t, at, :] for t in range(27)]
    for z in range(ZOUT):
        for parity in range(2):
            sums = {}
            for x in range(parity, limit, 2):
                rows = [cells[z + ZOUT * m, pl.ds(b * (ROWS * slots) + x, ROWS, stride=slots), :] for m in range(3)]
                for m in range(3):
                    for dx in (1, 0, -1):
                        out = x - 2 * dx
                        if 0 <= out < limit:
                            for dy in (-1, 0, 1):
                                term = tap[tap_of(m, dx, dy)] * rows[m]
                                key = (out, dy)
                                sums[key] = sums[key] + term if key in sums else term
                for out in [x - 2] if x + 2 < limit else [x - 2, x]:
                    if out >= 0:
                        depth[z, out, at, :] = shifted_sum(*(sums.pop((out, dy)) for dy in (-1, 0, 1)))


def outer_kernel(widths, weights, coarse, cells_in, cells, rims, own_block):
    width = widths[lax.axis_index("gx")]
    channels, tile = weights.shape[1:]
    slots = cells.shape[1] // channels
    own_block[...] = coarse[...]
    for b in range(channels // ROWS):
        at = slice(b * ROWS, (b + 1) * ROWS)
        for side, dx in enumerate((1, -1)):
            tap = [[weights[tap_of(m, dx, dy), at, :] for m in range(3)] for dy in (-1, 0, 1)]
            for r in range(2):
                x = r if side == 0 else width - 2 + r
                for z in range(ZOUT):
                    rows = [
                        cells[z + ZOUT * m, pl.ds(b * (ROWS * slots) + x, ROWS, stride=slots), :] for m in range(3)
                    ]
                    parts = [sum(weight * row for weight, row in zip(weights_of, rows)) for weights_of in tap]
                    rims[z, 2 * side + r, at, :] = shifted_sum(*parts)
    for r in range(2):

        @pl.when(width + r < slots)
        def _():
            for z in range(cells.shape[0]):
                cells[z, pl.ds(width + r, channels, stride=slots), :] = jnp.zeros((channels, tile), F32)


def conv_kernel(widths, edge, cells, weights, depth):
    width = widths[lax.axis_index("gx")]
    channels = weights.shape[1]
    slots = cells.shape[1] // channels
    for limit in range(ROWS, slots + 1, ROWS):

        @pl.when((width > limit - ROWS) & (width <= limit))
        def _():
            def convolve(b, carry):
                convolve_block(cells, weights, depth, b, limit)
                return carry

            lax.fori_loop(0, channels // ROWS, convolve, 0)


def edge_term(edge, z, x):
    tile = edge.shape[2]
    begin = 8 * (x & 15) + 4 * z
    cells = pltpu.roll(edge[(x >> 4) & 1], (tile - 2 - begin) & (tile - 1), 1)
    lane = lane_iota(cells.shape)
    return jnp.where((lane < 2) | (lane >= tile - 2), cells, 0.0)


def rim_kernel(widths, first, second, rims, edge, far, near):
    width = widths[lax.axis_index("gx")]
    _, _, channels, tile = rims.shape
    left, right = first[0:channels, :].astype(F32), second[0:channels, :].astype(F32)
    on_left = (lane_iota((channels, tile)) & 2) != 0
    edge[0] = jnp.where(on_left, pltpu.roll(left, 2, 1), pltpu.roll(right, tile - 2, 1))
    edge[1] = jnp.where(on_left, left, right)
    even = is_even("gx")
    for z in range(ZOUT):
        for r in range(2):
            to_lower = rims[z, r] + edge_term(edge, z, r - 2)
            to_upper = rims[z, 2 + r] + edge_term(edge, z, width + r)
            at = slice((2 * z + r) * channels, (2 * z + r + 1) * channels)
            near[at, :] = jnp.where(even, to_upper, to_lower).astype(BF16)
            far[at, :] = jnp.where(even, to_lower, to_upper).astype(BF16)


def slab_start(widths):
    slab = lax.axis_index("gx")
    start = jnp.int32(0)
    for d in range(widths.shape[0]):
        start = start + jnp.where(d < slab, widths[d], 0)
    return start


def depth_row(weights, depth, edge, z, x):
    return depth[z, x] + weights[DW_BIAS] + edge_term(edge, z, x)


def base_row(cells, lifted, phase, z, x):
    channels = lifted.shape[1]
    slots = cells.shape[1] // channels
    return cells[2 + z, pl.ds(x, channels, stride=slots), :] + lifted[lax.div(phase + x, CF)]


def active(weights, mixed):
    mixed = mixed + weights[PW_BIAS]
    return jnp.maximum(mixed, 0.2 * mixed)


def mix_kernel(gathered, widths, mix, cells, weights, depth, edge, *refs):
    if gathered:
        coarse, value, ends, bases, lifted, across, mixer = refs
        parts, ncx, ncy = coarse.shape
    else:
        first, second, own_block, opposite, value, ends, bases, lifted, across, mixer, blocks = refs
        parts, own_rows, ncy = own_block.shape
        ncx = 4 * own_rows
    width = widths[lax.axis_index("gx")]
    here = lax.axis_index("gy")
    start = slab_start(widths)
    phase = lax.rem(start, CF)
    channels, tile = weights.shape[1:]
    slots = cells.shape[1] // channels

    if not gathered:
        count = parts * own_rows
        for message, owner in ((first, lax.rem(here + 3, 4)), (second, lax.rem(here + 1, 4))):
            terms = message[channels:, :].astype(F32)[0:count, :]
            sums = terms[:, 0:ncy] + terms[:, ncy : 2 * ncy] + terms[:, 2 * ncy : 3 * ncy]
            for k in range(parts):
                blocks[k, pl.ds(owner * own_rows, own_rows), :] = sums[k * own_rows : (k + 1) * own_rows]
        for block, owner in ((own_block, here), (opposite, lax.rem(here + 2, 4))):
            for k in range(parts):
                blocks[k, pl.ds(owner * own_rows, own_rows), :] = block[k]
    shape = (ncy, tile)
    cell = row_iota(shape) * CF
    place = lane_iota(shape) + here * tile
    along_y = ((place >= cell) & (place < cell + CF)).astype(F32)
    for k in range(parts):
        block = coarse[k] if gathered else blocks[k]
        across[k] = jnp.dot(block, along_y, precision=lax.Precision.HIGHEST, preferred_element_type=F32)
    for i in range(3):
        cell = lax.rem(lax.div(start, CF) + i, ncx)
        total = None
        for k in range(parts):
            term = weights[LIFT + k] * across[k, pl.ds(cell, 1), :]
            total = term if total is None else total + term
        lifted[i] = total

    group = 4
    wide = jnp.concatenate([mix[...]] * group, axis=1)
    wide = jnp.concatenate([wide] * group, axis=0)
    size = group * channels
    row, column = row_iota((size, size)), lane_iota((size, size))
    same = sum(
        ((row >= i * channels) & (row < (i + 1) * channels) & (column >= i * channels) & (column < (i + 1) * channels)).astype(F32)
        for i in range(group)
    )
    mixer[...] = jnp.where(same > 0, wide.astype(F32), 0.0).astype(BF16)

    def mix_rows(limit):
        for x in range(0, limit, group):
            depths = [
                jnp.concatenate([depth_row(weights, depth, edge, z, x + i) for i in range(group)], axis=0)
                for z in range(ZOUT)
            ]
            mixed = jnp.dot(mixer[...], jnp.concatenate(depths, axis=1).astype(BF16), preferred_element_type=F32)
            for i in range(group):
                for z in range(ZOUT):
                    part = mixed[i * channels : (i + 1) * channels, z * tile : (z + 1) * tile]
                    part = active(weights, part) + base_row(cells, lifted, phase, z, x + i)
                    if x + i >= limit - ROWS:
                        part = jnp.where(x + i < width, part, 0.0)
                    value[z, pl.ds(x + i, channels, stride=slots), :] = part
        for x in range(limit, slots):
            for z in range(ZOUT):
                value[z, pl.ds(x, channels, stride=slots), :] = jnp.zeros((channels, tile), F32)
        for z in range(ZOUT):
            for i, x in enumerate((0, 1, width - 2, width - 1)):
                ends[z, i] = depth_row(weights, depth, edge, z, x)
                bases[z, i] = base_row(cells, lifted, phase, z, x)

    for limit in range(ROWS, slots + 1, ROWS):
        pl.when((width > limit - ROWS) & (width <= limit))(lambda limit=limit: mix_rows(limit))


def finish_kernel(widths, mix, weights, ends, bases, far, near, value_in, out, value, block, sems):
    width = widths[lax.axis_index("gx")]
    channels, tile = weights.shape[1:]
    slots = block.shape[2]
    even = is_even("gx")
    mixed = []
    for z in range(ZOUT):
        sums = []
        for i in range(4):
            at = slice((2 * z + i % 2) * channels, (2 * z + i % 2 + 1) * channels)
            one, two = far[at, :].astype(F32), near[at, :].astype(F32)
            arrived = jnp.where(even, one, two) if i < 2 else jnp.where(even, two, one)
            sums.append((ends[z, i] + arrived).astype(BF16))
        mixed.append(jnp.dot(mix[...], jnp.concatenate(sums, axis=1), preferred_element_type=F32))
    copies = []
    for z in range(ZOUT):
        for part in range(channels // CHUNK):
            at = slice(part * CHUNK, (part + 1) * CHUNK)
            for i, x in enumerate((0, 1, width - 2, width - 1)):
                rows = mixed[z][at, i * tile : (i + 1) * tile] + weights[PW_BIAS, at, :]
                rows = jnp.maximum(rows, 0.2 * rows) + bases[z, i, at, :]
                value[z, pl.ds(part * CHUNK * slots + x, CHUNK, stride=slots), :] = rows
            for o in range(part * CHUNK, (part + 1) * CHUNK):
                block[z, o] = value[z, o * slots : (o + 1) * slots, :].astype(BF16)
            part_of = pl.ds(part * CHUNK, CHUNK)
            copy = pltpu.make_async_copy(block.at[z, part_of], out.at[z, part_of], sems.at[part, z])
            copy.start()
            copies.append(copy)
    for copy in copies:
        copy.wait()


def shards(feature, widths, dw_weight, dw_bias, pw_weight, pw_bias, lift_weight, coarse):
    planes, channels, slots, tile = feature.shape
    ny = lax.axis_size("gy")
    parts, own_rows, ncy = coarse.shape
    gathered = ny != 4
    ncx = ny * own_rows
    smem = pl.BlockSpec(memory_space=pltpu.SMEM)
    vmem = pl.BlockSpec(memory_space=pltpu.VMEM)
    hbm = pl.BlockSpec(memory_space=pltpu.HBM)
    params = pltpu.CompilerParams(vmem_limit_bytes=VMEM_BYTES)
    shape = jax.ShapeDtypeStruct
    strip = shape((channels + 16, tile), BF16)
    cells_shape = pltpu.VMEM((planes, channels * slots, tile), F32)
    value_shape = pltpu.VMEM((ZOUT, channels * slots, tile), F32)
    message = shape((2 * ZOUT * channels, tile), BF16)

    def swapped(array, axis, first):
        count = lax.axis_size(axis)
        pairs = []
        for i in range(first, count + first, 2):
            a, b = i % count, (i + 1) % count
            pairs += [(a, b), (b, a)]
        return lax.ppermute(array, axis, pairs)

    def pinned(array):
        return pltpu.with_memory_space_constraint(array, pltpu.HBM)

    if gathered:
        every = lax.all_gather(coarse, "gy", axis=1, tiled=True)
    small = (
        widths,
        dw_weight,
        dw_bias.reshape(1, channels),
        pw_bias.reshape(1, channels),
        lift_weight.T,
        coarse,
    )
    cells, weights, first, second, block, slab_widths = pl.pallas_call(
        pack_kernel,
        out_shape=(
            cells_shape,
            pltpu.VMEM((32, channels, tile), F32),
            strip,
            strip,
            pltpu.VMEM(coarse.shape, F32),
            pltpu.SMEM(widths.shape, jnp.int32),
        ),
        in_specs=[hbm] * 7,
        out_specs=(vmem,) * 5 + (smem,),
        scratch_shapes=[
            pltpu.VMEM(feature.shape, BF16),
            pltpu.SMEM(widths.shape, jnp.int32),
            pltpu.VMEM(dw_weight.shape, F32),
            pltpu.VMEM((1, channels), F32),
            pltpu.VMEM((1, channels), F32),
            pltpu.VMEM((parts, channels), F32),
            pltpu.VMEM(coarse.shape, F32),
            pltpu.VMEM((32, channels), F32),
            pltpu.VMEM((16, tile), F32),
            pltpu.VMEM((3, 2, channels, tile), F32),
            pltpu.SemaphoreType.DMA((3, 2)),
            pltpu.SemaphoreType.DMA((len(small),)),
        ],
        compiler_params=params,
    )(pinned(feature), *(pinned(array) for array in small))
    first = lax.ppermute(first, "gy", [(i, (i + 1) % ny) for i in range(ny)])
    second = lax.ppermute(second, "gy", [((i + 1) % ny, i) for i in range(ny)])
    cells, rims, own_block = pl.pallas_call(
        outer_kernel,
        out_shape=(
            cells_shape,
            pltpu.VMEM((ZOUT, 4, channels, tile), F32),
            pltpu.VMEM(coarse.shape, F32),
        ),
        in_specs=[smem] + [vmem] * 3,
        out_specs=(vmem,) * 3,
        input_output_aliases={3: 0},
        compiler_params=params,
        cost_estimate=pl.CostEstimate(flops=10**8, bytes_accessed=10**6, transcendentals=0),
    )(slab_widths, weights, block, cells)
    if not gathered:
        opposite = lax.ppermute(own_block, "gy", [(i, (i + 2) % 4) for i in range(4)])
    edge, far, near = pl.pallas_call(
        rim_kernel,
        out_shape=(pltpu.VMEM((2, channels, tile), F32), message, message),
        in_specs=[smem] + [vmem] * 3,
        out_specs=(vmem,) * 3,
        compiler_params=params,
    )(slab_widths, first, second, rims)
    far = swapped(far, "gx", 1)
    near = swapped(near, "gx", 0)
    blocks = (every,) if gathered else (first, second, own_block, opposite)
    depth = pl.pallas_call(
        conv_kernel,
        out_shape=pltpu.VMEM((ZOUT, slots, channels, tile), F32),
        in_specs=[smem] + [vmem] * 3,
        out_specs=vmem,
        compiler_params=params,
        cost_estimate=pl.CostEstimate(flops=10**9, bytes_accessed=10**6, transcendentals=0),
    )(slab_widths, edge, cells, weights)
    ends_shape = pltpu.VMEM((ZOUT, 4, channels, tile), F32)
    value, ends, bases = pl.pallas_call(
        functools.partial(mix_kernel, gathered),
        out_shape=(value_shape, ends_shape, ends_shape),
        in_specs=[smem] + [vmem] * (5 + len(blocks)),
        out_specs=(vmem,) * 3,
        scratch_shapes=[
            pltpu.VMEM((3, channels, tile), F32),
            pltpu.VMEM((parts, ncx, tile), F32),
            pltpu.VMEM((4 * channels, 4 * channels), BF16),
        ]
        + ([] if gathered else [pltpu.VMEM((parts, ncx, ncy), F32)]),
        compiler_params=params,
        cost_estimate=pl.CostEstimate(flops=10**9, bytes_accessed=10**6, transcendentals=0),
    )(slab_widths, pw_weight, cells, weights, depth, edge, *blocks)
    out, _ = pl.pallas_call(
        finish_kernel,
        out_shape=(shape((ZOUT, channels, slots, tile), BF16), value_shape),
        in_specs=[smem] + [vmem] * 7,
        out_specs=(hbm, vmem),
        scratch_shapes=[
            pltpu.VMEM((ZOUT, channels, slots, tile), BF16),
            pltpu.SemaphoreType.DMA((channels // CHUNK, ZOUT)),
        ],
        input_output_aliases={7: 1},
        compiler_params=params,
    )(slab_widths, pw_weight, weights, ends, bases, far, near, value)
    return out


def solution(mesh):
    placed = (P(None, None, "gx", "gy"), P(), P(), P(), P(), P(), P(), P(None, "gy", None))
    return jax.shard_map(
        shards, mesh=mesh, in_specs=placed, out_specs=P(None, None, "gx", "gy"), check_vma=False
    )
```

profile of v0, /device:TPU:3, one launch (start us, length us, event | category | flops | bytes accessed | tf_op | source)
XLA Modules:
  0.0 17.5 jit_solution(16389741375465548194)
XLA Ops:
  0.0 2.9 %shard_map.82 = (f32[6,1536,128]{2,1,0:T(8,128)S(1)}, f32[32,64,128]{2,1,0:T(8,128)S(1)}, bf16[80,128]{1,0:T(8,128)(2,1)S(1)}, bf16[80,128]{1,0:T(8,128)(2,1)S(1...) custom-call(bf16[6,64,24,128]{3,2,1,0:T(8,128)(2,1)} %feature.1, s32[8]{0:T(128)} %widths_in.1, f32[27,64]{1,0:T(8,128)} %taps_in.1, ...), custom_call_target="tpu_custom_call" | custom-call | tf_op jit(solution)/shard_map/pallas_call | solution.py:426
  3.0 1.3 %collective-permute-start = (bf16[80,128]{1,0:T(8,128)(2,1)S(1)}, bf16[80,128]{1,0:T(8,128)(2,1)S(1)}, u32[]{:S(2)}, u32[]{:S(2)}) collective-permute-start(bf16[80,128]{1,0:T(8,128)(2,1)S(1)} %get-tuple-element.26), channel_id=1, source_target_pairs={{0,1},{1,2},{2,3},{3,0},{4,5},{5,6},{6,7},{7,4},{8,9},{9,10},{10,1... | collective-permute-start | bytes 61448 | tf_op jit(solution)/shard_map/ppermute | solution.py:454
  4.2 0.3 %collective-permute-start.1 = (bf16[80,128]{1,0:T(8,128)(2,1)S(1)}, bf16[80,128]{1,0:T(8,128)(2,1)S(1)}, u32[]{:S(2)}, u32[]{:S(2)}) collective-permute-start(bf16[80,128]{1,0:T(8,128)(2,1)S(1)} %get-tuple-element.27), channel_id=1, source_target_pairs={{1,0},{2,1},{3,2},{0,3},{5,4},{6,5},{7,6},{4,7},{9,8},{10,9},{11,1... | collective-permute-start | bytes 61448 | tf_op jit(solution)/shard_map/ppermute | solution.py:455
  4.5 0.4 %shard_map.83 = (f32[6,1536,128]{2,1,0:T(8,128)S(1)}, f32[2,4,64,128]{3,2,1,0:T(8,128)S(1)}, f32[3,2,32]{2,1,0:T(2,128)S(1)}) custom-call(s32[8]{0:T(128)S(4)} %get-tuple-element.21.widths, f32[32,64,128]{2,1,0:T(8,128)S(1)} %get-tuple-element.22.weights, f32[3,2,32]{2,1,0:T(2,128)S(1)} %get-tuple-element.23.coarse, ...), custom_call_target="tpu_custom_call", output_to_operand_aliasing={{0}: (3, {})} | custom-call | flops 100000000 | bytes 1000000 | tf_op jit(solution)/shard_map/pallas_call | solution.py:456
  4.8 1.3 %collective-permute-start.2 = (f32[3,2,32]{2,1,0:T(2,128)S(1)}, f32[3,2,32]{2,1,0:T(2,128)S(1)}, u32[]{:S(2)}, u32[]{:S(2)}) collective-permute-start(f32[3,2,32]{2,1,0:T(2,128)S(1)} %get-tuple-element.30.refs_2_), channel_id=1, source_target_pairs={{0,2},{1,3},{2,0},{3,1},{4,6},{5,7},{6,4},{7,5},{8,10},{9,11},{10,... | collective-permute-start | bytes 2312 | tf_op jit(solution)/shard_map/ppermute | solution.py:470
  6.1 0.0 collective-permute-done.first.refs_0_
  6.2 1.8 %collective-permute-done.1.second.refs_1_ = bf16[80,128]{1,0:T(8,128)(2,1)S(1)} collective-permute-done((bf16[80,128]{1,0:T(8,128)(2,1)S(1)}, bf16[80,128]{1,0:T(8,128)(2,1)S(1)}, u32[]{:S(2)}, u32[]{:S(2)}) %collective-permute-start.1) | collective-permute-done | bytes 20512 | tf_op jit(solution)/shard_map/ppermute | solution.py:455
  7.9 0.2 %shard_map.84 = (f32[2,64,128]{2,1,0:T(8,128)S(1)}, bf16[256,128]{1,0:T(8,128)(2,1)S(1)}, bf16[256,128]{1,0:T(8,128)(2,1)S(1)}) custom-call(s32[8]{0:T(128)S(4)} %get-tuple-element.21.widths, bf16[80,128]{1,0:T(8,128)(2,1)S(1)} %collective-permute-done.first.refs_0_, bf16[80,128]{1,0:T(8,128)(2,1)S(1)} %collective-permute-done.1.second.refs_1_, ...), custom_call_target="tpu_custom_call" | custom-call | tf_op jit(solution)/shard_map/pallas_call | solution.py:471
  8.1 3.2 %collective-permute-start.3 = (bf16[256,128]{1,0:T(8,128)(2,1)S(1)}, bf16[256,128]{1,0:T(8,128)(2,1)S(1)}, u32[]{:S(2)}, u32[]{:S(2)}) collective-permute-start(bf16[256,128]{1,0:T(8,128)(2,1)S(1)} %get-tuple-element.33), channel_id=1, source_target_pairs={{4,8},{8,4},{12,16},{16,12},{20,24},{24,20},{28,0},{0,28},{5,9},{9... | collective-permute-start | bytes 196616 | tf_op jit(solution)/shard_map/ppermute | solution.py:411
  11.3 0.6 %collective-permute-start.4 = (bf16[256,128]{1,0:T(8,128)(2,1)S(1)}, bf16[256,128]{1,0:T(8,128)(2,1)S(1)}, u32[]{:S(2)}, u32[]{:S(2)}) collective-permute-start(bf16[256,128]{1,0:T(8,128)(2,1)S(1)} %get-tuple-element.34), channel_id=1, source_target_pairs={{0,4},{4,0},{8,12},{12,8},{16,20},{20,16},{24,28},{28,24},{1,5},{5... | collective-permute-start | bytes 196616 | tf_op jit(solution)/shard_map/ppermute | solution.py:411
  11.9 0.0 copy-start
  11.9 3.0 %shard_map.85.depth = f32[2,24,64,128]{3,2,1,0:T(8,128)S(1)} custom-call(s32[8]{0:T(128)S(4)} %get-tuple-element.21.widths, f32[2,64,128]{2,1,0:T(8,128)S(1)} %get-tuple-element.29.edge, f32[6,1536,128]{2,1,0:T(8,128)S(1)} %get-tuple-element.25.cells, f32[32,64,128]{2,1,0:T(8,128)S(1)} %get-tuple-element.22.weights), custom_call_target="tpu_custom_call" | custom-call | flops 1000000000 | bytes 1000000 | tf_op jit(solution)/shard_map/pallas_call | solution.py:481
  14.9 0.0 collective-permute-done.2.refs_3_
  14.9 0.0 copy-done
  14.9 1.4 %shard_map.86 = (f32[2,1536,128]{2,1,0:T(8,128)S(1)}, f32[2,4,64,128]{3,2,1,0:T(8,128)S(1)}, f32[2,4,64,128]{3,2,1,0:T(8,128)S(1)}) custom-call(s32[8]{0:T(128)S(4)} %get-tuple-element.21.widths, bf16[64,64]{1,0:T(8,128)(2,1)S(1)} %copy-done, f32[6,1536,128]{2,1,0:T(8,128)S(1)} %get-tuple-element.25.cells, f32[32,64,128]{2,1,0:T(8,128)S(1)} %get-tuple-element.22.weights, ...), custom_call_target="tpu_custom_call" | custom-call | flops 1000000000 | bytes 1000000 | tf_op jit(solution)/shard_map/pallas_call | solution.py:490
  16.3 0.0 collective-permute-done.3.far
  16.4 0.0 collective-permute-done.4.near
  16.4 1.1 %shard_map.87 = (bf16[2,64,24,128]{3,2,1,0:T(8,128)(2,1)}, f32[2,1536,128]{2,1,0:T(8,128)S(1)}) custom-call(s32[8]{0:T(128)S(4)} %get-tuple-element.21.widths, bf16[64,64]{1,0:T(8,128)(2,1)S(1)} %copy-done, f32[32,64,128]{2,1,0:T(8,128)S(1)} %get-tuple-element.22.weights, ...), custom_call_target="tpu_custom_call", output_to_operand_aliasing={{1}: (7, {})} | custom-call | tf_op jit(solution)/shard_map/pallas_call | solution.py:504
Async XLA Ops:
  3.0 3.2 %collective-permute-start = (bf16[80,128]{1,0:T(8,128)(2,1)S(1)}, bf16[80,128]{1,0:T(8,128)(2,1)S(1)}, u32[]{:S(2)}, u32[]{:S(2)}) collective-permute-start(bf16[80,128]{1,0:T(8,128)(2,1)S(1)} %get-tuple-element.26), channel_id=1, source_target_pairs={{0,1},{1,2},{2,3},{3,0},{4,5},{5,6},{6,7},{7,4},{8,9},{9,10},{10,1... | collective-permute-start | bytes 61448 | tf_op jit(solution)/shard_map/ppermute | solution.py:454
  4.2 3.7 %collective-permute-start.1 = (bf16[80,128]{1,0:T(8,128)(2,1)S(1)}, bf16[80,128]{1,0:T(8,128)(2,1)S(1)}, u32[]{:S(2)}, u32[]{:S(2)}) collective-permute-start(bf16[80,128]{1,0:T(8,128)(2,1)S(1)} %get-tuple-element.27), channel_id=1, source_target_pairs={{1,0},{2,1},{3,2},{0,3},{5,4},{6,5},{7,6},{4,7},{9,8},{10,9},{11,1... | collective-permute-start | bytes 61448 | tf_op jit(solution)/shard_map/ppermute | solution.py:455
  4.8 10.1 %collective-permute-start.2 = (f32[3,2,32]{2,1,0:T(2,128)S(1)}, f32[3,2,32]{2,1,0:T(2,128)S(1)}, u32[]{:S(2)}, u32[]{:S(2)}) collective-permute-start(f32[3,2,32]{2,1,0:T(2,128)S(1)} %get-tuple-element.30.refs_2_), channel_id=1, source_target_pairs={{0,2},{1,3},{2,0},{3,1},{4,6},{5,7},{6,4},{7,5},{8,10},{9,11},{10,... | collective-permute-start | bytes 2312 | tf_op jit(solution)/shard_map/ppermute | solution.py:470
  8.1 8.2 %collective-permute-start.3 = (bf16[256,128]{1,0:T(8,128)(2,1)S(1)}, bf16[256,128]{1,0:T(8,128)(2,1)S(1)}, u32[]{:S(2)}, u32[]{:S(2)}) collective-permute-start(bf16[256,128]{1,0:T(8,128)(2,1)S(1)} %get-tuple-element.33), channel_id=1, source_target_pairs={{4,8},{8,4},{12,16},{16,12},{20,24},{24,20},{28,0},{0,28},{5,9},{9... | collective-permute-start | bytes 196616 | tf_op jit(solution)/shard_map/ppermute | solution.py:411
  11.3 5.1 %collective-permute-start.4 = (bf16[256,128]{1,0:T(8,128)(2,1)S(1)}, bf16[256,128]{1,0:T(8,128)(2,1)S(1)}, u32[]{:S(2)}, u32[]{:S(2)}) collective-permute-start(bf16[256,128]{1,0:T(8,128)(2,1)S(1)} %get-tuple-element.34), channel_id=1, source_target_pairs={{0,4},{4,0},{8,12},{12,8},{16,20},{20,16},{24,28},{28,24},{1,5},{5... | collective-permute-start | bytes 196616 | tf_op jit(solution)/shard_map/ppermute | solution.py:411
  11.9 3.0 %copy-start = (bf16[64,64]{1,0:T(8,128)(2,1)S(1)}, bf16[64,64]{1,0:T(8,128)(2,1)}, u32[]{:S(2)}) copy-start(bf16[64,64]{1,0:T(8,128)(2,1)} %mix.3) | copy-start | bytes 24580
where the time goes:
time: 17.6 us; the launch traced here: 17.5 us
  Pallas kernels  9.01 us (51%)
  starting transfers between devices  6.6 us (38%)
  waiting for transfers between devices  1.81 us (10%)
    ppermute x2, starting transfers between devices, swapped(): return lax.ppermute(array, axis, pairs)  3.78 us
    pallas_call x1, Pallas kernels, shards(): pl.pallas_call(conv_kernel, out_shape=pltpu.VMEM((ZOUT, slots, channels,...  2.98 us
    pallas_call x1, Pallas kernels, shards(): pl.pallas_call(pack_kernel, out_shape=(cells_shape, pltpu.VMEM((32, chann...  2.94 us
    ppermute x1, waiting for transfers between devices, shards(): second = lax.ppermute(second, 'gy', [((i + 1) % ny, i) for i in range(ny)])  1.79 us
    pallas_call x1, Pallas kernels, shards(): pl.pallas_call(functools.partial(mix_kernel, gathered), out_shape=(value_...  1.41 us
    ppermute x1, starting transfers between devices, shards(): lax.ppermute(own_block, 'gy', [(i, (i + 2) % 4) for i in range(4)])  1.3 us
    ppermute x1, starting transfers between devices, shards(): first = lax.ppermute(first, 'gy', [(i, (i + 1) % ny) for i in range(ny)])  1.26 us
    pallas_call x1, Pallas kernels, shards(): pl.pallas_call(finish_kernel, out_shape=(shape((ZOUT, channels, slots, ti...  1.13 us
  transfers between devices with their start and end apart: 5, of which 1 were waited for; matrix products, arithmetic and copies ran while one was open for 0% of the time, Pallas kernels for 28%

commit v1 on v0

--- a/solution.py
+++ b/solution.py
@@ -11,6 +11,7 @@
 ZOUT = 2
 CF = 16
 ROWS = 8
+SPLIT = 1
 CHUNK = 16
 DW_BIAS, PW_BIAS, LIFT = 27, 28, 29
 F32 = jnp.float32
@@ -166,10 +167,11 @@
     return centre + before + after
 
 
-def convolve_block(cells, weights, depth, b, limit):
+def convolve_block(cells, weights, depth, b, first, limit):
     channels = weights.shape[1]
     slots = cells.shape[1] // channels
     at = pl.ds(pl.multiple_of(b * ROWS, ROWS), ROWS)
+    to = pl.ds(pl.multiple_of((b - first) * ROWS, ROWS), ROWS)
     tap = [weights[t, at, :] for t in range(27)]
     for z in range(ZOUT):
         for parity in range(2):
@@ -186,7 +188,7 @@
                                 sums[key] = sums[key] + term if key in sums else term
                 for out in [x - 2] if x + 2 < limit else [x - 2, x]:
                     if out >= 0:
-                        depth[z, out, at, :] = shifted_sum(*(sums.pop((out, dy)) for dy in (-1, 0, 1)))
+                        depth[z, out, to, :] = shifted_sum(*(sums.pop((out, dy)) for dy in (-1, 0, 1)))
 
 
 def outer_kernel(widths, weights, coarse, cells_in, cells, rims, own_block):
@@ -214,19 +216,26 @@
                 cells[z, pl.ds(width + r, channels, stride=slots), :] = jnp.zeros((channels, tile), F32)
 
 
-def conv_kernel(widths, edge, cells, weights, depth):
+def convolve_blocks(widths, cells, weights, depth, first, last):
     width = widths[lax.axis_index("gx")]
-    channels = weights.shape[1]
-    slots = cells.shape[1] // channels
+    slots = cells.shape[1] // weights.shape[1]
     for limit in range(ROWS, slots + 1, ROWS):
 
         @pl.when((width > limit - ROWS) & (width <= limit))
         def _():
             def convolve(b, carry):
-                convolve_block(cells, weights, depth, b, limit)
+                convolve_block(cells, weights, depth, b, first, limit)
                 return carry
 
-            lax.fori_loop(0, channels // ROWS, convolve, 0)
+            lax.fori_loop(first, last, convolve, 0)
+
+
+def early_kernel(widths, cells, weights, depth):
+    convolve_blocks(widths, cells, weights, depth, 0, SPLIT)
+
+
+def rest_kernel(widths, edge, cells, weights, depth):
+    convolve_blocks(widths, cells, weights, depth, SPLIT, weights.shape[1] // ROWS)
 
 
 def edge_term(edge, z, x):
@@ -262,8 +271,9 @@
     return start
 
 
-def depth_row(weights, depth, edge, z, x):
-    return depth[z, x] + weights[DW_BIAS] + edge_term(edge, z, x)
+def depth_row(weights, depths, edge, z, x):
+    own = jnp.concatenate([depth[z, x] for depth in depths], axis=0)
+    return own + weights[DW_BIAS] + edge_term(edge, z, x)
 
 
 def base_row(cells, lifted, phase, z, x):
@@ -277,7 +287,7 @@
     return jnp.maximum(mixed, 0.2 * mixed)
 
 
-def mix_kernel(gathered, widths, mix, cells, weights, depth, edge, *refs):
+def mix_kernel(gathered, widths, mix, cells, weights, depth, rest, edge, *refs):
     if gathered:
         coarse, value, ends, bases, lifted, across, mixer = refs
         parts, ncx, ncy = coarse.shape
@@ -328,10 +338,10 @@
     )
     mixer[...] = jnp.where(same > 0, wide.astype(F32), 0.0).astype(BF16)
 
-    def mix_rows(limit):
-        for x in range(0, limit, group):
+    def mix_rows(begin, end):
+        for x in range(begin, end, group):
             depths = [
-                jnp.concatenate([depth_row(weights, depth, edge, z, x + i) for i in range(group)], axis=0)
+                jnp.concatenate([depth_row(weights, (depth, rest), edge, z, x + i) for i in range(group)], axis=0)
                 for z in range(ZOUT)
             ]
             mixed = jnp.dot(mixer[...], jnp.concatenate(depths, axis=1).astype(BF16), preferred_element_type=F32)
@@ -339,19 +349,24 @@
                 for z in range(ZOUT):
                     part = mixed[i * channels : (i + 1) * channels, z * tile : (z + 1) * tile]
                     part = active(weights, part) + base_row(cells, lifted, phase, z, x + i)
-                    if x + i >= limit - ROWS:
+                    if x + i >= end - ROWS and begin:
                         part = jnp.where(x + i < width, part, 0.0)
                     value[z, pl.ds(x + i, channels, stride=slots), :] = part
+
+    mix_rows(0, ROWS)
+    for z in range(ZOUT):
+        for i, x in enumerate((0, 1, width - 2, width - 1)):
+            ends[z, i] = depth_row(weights, (depth, rest), edge, z, x)
+            bases[z, i] = base_row(cells, lifted, phase, z, x)
+
+    def further_rows(limit):
+        mix_rows(ROWS, limit)
         for x in range(limit, slots):
             for z in range(ZOUT):
                 value[z, pl.ds(x, channels, stride=slots), :] = jnp.zeros((channels, tile), F32)
-        for z in range(ZOUT):
-            for i, x in enumerate((0, 1, width - 2, width - 1)):
-                ends[z, i] = depth_row(weights, depth, edge, z, x)
-                bases[z, i] = base_row(cells, lifted, phase, z, x)
 
     for limit in range(ROWS, slots + 1, ROWS):
-        pl.when((width > limit - ROWS) & (width <= limit))(lambda limit=limit: mix_rows(limit))
+        pl.when((width > limit - ROWS) & (width <= limit))(lambda limit=limit: further_rows(limit))
 
 
 def finish_kernel(widths, mix, weights, ends, bases, far, near, value_in, out, value, block, sems):
@@ -468,6 +483,15 @@
     )(slab_widths, weights, block, cells)
     if not gathered:
         opposite = lax.ppermute(own_block, "gy", [(i, (i + 2) % 4) for i in range(4)])
+    early = SPLIT * ROWS
+    depth = pl.pallas_call(
+        early_kernel,
+        out_shape=pltpu.VMEM((ZOUT, slots, early, tile), F32),
+        in_specs=[smem] + [vmem] * 2,
+        out_specs=vmem,
+        compiler_params=params,
+        cost_estimate=pl.CostEstimate(flops=10**9, bytes_accessed=10**6, transcendentals=0),
+    )(slab_widths, cells, weights)
     edge, far, near = pl.pallas_call(
         rim_kernel,
         out_shape=(pltpu.VMEM((2, channels, tile), F32), message, message),
@@ -478,9 +502,9 @@
     far = swapped(far, "gx", 1)
     near = swapped(near, "gx", 0)
     blocks = (every,) if gathered else (first, second, own_block, opposite)
-    depth = pl.pallas_call(
-        conv_kernel,
-        out_shape=pltpu.VMEM((ZOUT, slots, channels, tile), F32),
+    rest = pl.pallas_call(
+        rest_kernel,
+        out_shape=pltpu.VMEM((ZOUT, slots, channels - early, tile), F32),
         in_specs=[smem] + [vmem] * 3,
         out_specs=vmem,
         compiler_params=params,
@@ -490,7 +514,7 @@
     value, ends, bases = pl.pallas_call(
         functools.partial(mix_kernel, gathered),
         out_shape=(value_shape, ends_shape, ends_shape),
-        in_specs=[smem] + [vmem] * (5 + len(blocks)),
+        in_specs=[smem] + [vmem] * (6 + len(blocks)),
         out_specs=(vmem,) * 3,
         scratch_shapes=[
             pltpu.VMEM((3, channels, tile), F32),
@@ -500,7 +524,7 @@
         + ([] if gathered else [pltpu.VMEM((parts, ncx, ncy), F32)]),
         compiler_params=params,
         cost_estimate=pl.CostEstimate(flops=10**9, bytes_accessed=10**6, transcendentals=0),
-    )(slab_widths, pw_weight, cells, weights, depth, edge, *blocks)
+    )(slab_widths, pw_weight, cells, weights, depth, rest, edge, *blocks)
     out, _ = pl.pallas_call(
         finish_kernel,
         out_shape=(shape((ZOUT, channels, slots, tile), BF16), value_shape),

time: 17.6 us -> 17.5 us (level)
  the two profiles are of different devices: /device:TPU:3 before, /device:TPU:1 now
where the time goes in v1:
time: 17.5 us; the launch traced here: 17.4 us
  Pallas kernels  8.84 us (51%)
  starting transfers between devices  8.43 us (48%)
    ppermute x2, starting transfers between devices, swapped(): return lax.ppermute(array, axis, pairs)  3.87 us
    pallas_call x1, Pallas kernels, shards(): pl.pallas_call(pack_kernel, out_shape=(cells_shape, pltpu.VMEM((32, chann...  2.94 us
    pallas_call x1, Pallas kernels, shards(): pl.pallas_call(rest_kernel, out_shape=pltpu.VMEM((ZOUT, slots, channels -...  2.59 us
    ppermute x1, starting transfers between devices, shards(): first = lax.ppermute(first, 'gy', [(i, (i + 1) % ny) for i in range(ny)])  2.09 us
    ppermute x1, starting transfers between devices, shards(): lax.ppermute(own_block, 'gy', [(i, (i + 2) % 4) for i in range(4)])  1.44 us
    pallas_call x1, Pallas kernels, shards(): pl.pallas_call(functools.partial(mix_kernel, gathered), out_shape=(value_...  1.33 us
    pallas_call x1, Pallas kernels, shards(): pl.pallas_call(finish_kernel, out_shape=(shape((ZOUT, channels, slots, ti...  1.13 us
    ppermute x1, starting transfers between devices, shards(): second = lax.ppermute(second, 'gy', [((i + 1) % ny, i) for i in range(ny)])  1.02 us
  transfers between devices with their start and end apart: 5, of which 0 were waited for; matrix products, arithmetic and copies ran while one was open for 0% of the time, Pallas kernels for 27%

profile of v1, /device:TPU:1, one launch (start us, length us, event | category | flops | bytes accessed | tf_op | source)
XLA Modules:
  0.0 17.4 jit_solution(14473293594031276832)
XLA Ops:
  0.0 2.9 %shard_map.82 = (f32[6,1536,128]{2,1,0:T(8,128)S(1)}, f32[32,64,128]{2,1,0:T(8,128)S(1)}, bf16[80,128]{1,0:T(8,128)(2,1)S(1)}, bf16[80,128]{1,0:T(8,128)(2,1)S(1...) custom-call(bf16[6,64,24,128]{3,2,1,0:T(8,128)(2,1)} %feature.1, s32[8]{0:T(128)} %widths_in.1, f32[27,64]{1,0:T(8,128)} %taps_in.1, ...), custom_call_target="tpu_custom_call" | custom-call | tf_op jit(solution)/shard_map/pallas_call | solution.py:441
  3.0 2.1 %collective-permute-start = (bf16[80,128]{1,0:T(8,128)(2,1)S(1)}, bf16[80,128]{1,0:T(8,128)(2,1)S(1)}, u32[]{:S(2)}, u32[]{:S(2)}) collective-permute-start(bf16[80,128]{1,0:T(8,128)(2,1)S(1)} %get-tuple-element.26), channel_id=1, source_target_pairs={{0,1},{1,2},{2,3},{3,0},{4,5},{5,6},{6,7},{7,4},{8,9},{9,10},{10,1... | collective-permute-start | bytes 61448 | tf_op jit(solution)/shard_map/ppermute | solution.py:469
  5.0 1.0 %collective-permute-start.1 = (bf16[80,128]{1,0:T(8,128)(2,1)S(1)}, bf16[80,128]{1,0:T(8,128)(2,1)S(1)}, u32[]{:S(2)}, u32[]{:S(2)}) collective-permute-start(bf16[80,128]{1,0:T(8,128)(2,1)S(1)} %get-tuple-element.27), channel_id=1, source_target_pairs={{1,0},{2,1},{3,2},{0,3},{5,4},{6,5},{7,6},{4,7},{9,8},{10,9},{11,1... | collective-permute-start | bytes 61448 | tf_op jit(solution)/shard_map/ppermute | solution.py:470
  6.1 0.3 %shard_map.83 = (f32[6,1536,128]{2,1,0:T(8,128)S(1)}, f32[2,4,64,128]{3,2,1,0:T(8,128)S(1)}, f32[3,2,32]{2,1,0:T(2,128)S(1)}) custom-call(s32[8]{0:T(128)S(4)} %get-tuple-element.21.widths, f32[32,64,128]{2,1,0:T(8,128)S(1)} %get-tuple-element.22.weights, f32[3,2,32]{2,1,0:T(2,128)S(1)} %get-tuple-element.23.coarse, ...), custom_call_target="tpu_custom_call", output_to_operand_aliasing={{0}: (3, {})} | custom-call | flops 100000000 | bytes 1000000 | tf_op jit(solution)/shard_map/pallas_call | solution.py:471
  6.4 1.4 %collective-permute-start.2 = (f32[3,2,32]{2,1,0:T(2,128)S(1)}, f32[3,2,32]{2,1,0:T(2,128)S(1)}, u32[]{:S(2)}, u32[]{:S(2)}) collective-permute-start(f32[3,2,32]{2,1,0:T(2,128)S(1)} %get-tuple-element.30.refs_2_), channel_id=1, source_target_pairs={{0,2},{1,3},{2,0},{3,1},{4,6},{5,7},{6,4},{7,5},{8,10},{9,11},{10,... | collective-permute-start | bytes 2312 | tf_op jit(solution)/shard_map/ppermute | solution.py:485
  7.8 0.4 %shard_map.84.depth = f32[2,24,8,128]{3,2,1,0:T(8,128)S(1)} custom-call(s32[8]{0:T(128)S(4)} %get-tuple-element.21.widths, f32[6,1536,128]{2,1,0:T(8,128)S(1)} %get-tuple-element.25.cells, f32[32,64,128]{2,1,0:T(8,128)S(1)} %get-tuple-element.22.weights), custom_call_target="tpu_custom_call" | custom-call | flops 1000000000 | bytes 1000000 | tf_op jit(solution)/shard_map/pallas_call | solution.py:487
  8.2 0.0 collective-permute-done.first.refs_0_
  8.2 0.0 collective-permute-done.1.second.refs_1_
  8.2 0.2 %shard_map.85 = (f32[2,64,128]{2,1,0:T(8,128)S(1)}, bf16[256,128]{1,0:T(8,128)(2,1)S(1)}, bf16[256,128]{1,0:T(8,128)(2,1)S(1)}) custom-call(s32[8]{0:T(128)S(4)} %get-tuple-element.21.widths, bf16[80,128]{1,0:T(8,128)(2,1)S(1)} %collective-permute-done.first.refs_0_, bf16[80,128]{1,0:T(8,128)(2,1)S(1)} %collective-permute-done.1.second.refs_1_, ...), custom_call_target="tpu_custom_call" | custom-call | tf_op jit(solution)/shard_map/pallas_call | solution.py:495
  8.4 2.8 %collective-permute-start.3 = (bf16[256,128]{1,0:T(8,128)(2,1)S(1)}, bf16[256,128]{1,0:T(8,128)(2,1)S(1)}, u32[]{:S(2)}, u32[]{:S(2)}) collective-permute-start(bf16[256,128]{1,0:T(8,128)(2,1)S(1)} %get-tuple-element.33), channel_id=1, source_target_pairs={{4,8},{8,4},{12,16},{16,12},{20,24},{24,20},{28,0},{0,28},{5,9},{9... | collective-permute-start | bytes 196616 | tf_op jit(solution)/shard_map/ppermute | solution.py:426
  11.2 1.0 %collective-permute-start.4 = (bf16[256,128]{1,0:T(8,128)(2,1)S(1)}, bf16[256,128]{1,0:T(8,128)(2,1)S(1)}, u32[]{:S(2)}, u32[]{:S(2)}) collective-permute-start(bf16[256,128]{1,0:T(8,128)(2,1)S(1)} %get-tuple-element.34), channel_id=1, source_target_pairs={{0,4},{4,0},{8,12},{12,8},{16,20},{20,16},{24,28},{28,24},{1,5},{5... | collective-permute-start | bytes 196616 | tf_op jit(solution)/shard_map/ppermute | solution.py:426
  12.3 0.0 copy-start
  12.3 2.6 %shard_map.86.rest = f32[2,24,56,128]{3,2,1,0:T(8,128)S(1)} custom-call(s32[8]{0:T(128)S(4)} %get-tuple-element.21.widths, f32[2,64,128]{2,1,0:T(8,128)S(1)} %get-tuple-element.29.edge, f32[6,1536,128]{2,1,0:T(8,128)S(1)} %get-tuple-element.25.cells, f32[32,64,128]{2,1,0:T(8,128)S(1)} %get-tuple-element.22.weights), custom_call_target="tpu_custom_call" | custom-call | flops 1000000000 | bytes 1000000 | tf_op jit(solution)/shard_map/pallas_call | solution.py:505
  14.9 0.0 collective-permute-done.2.refs_3_
  14.9 0.0 copy-done
  14.9 1.3 %shard_map.87 = (f32[2,1536,128]{2,1,0:T(8,128)S(1)}, f32[2,4,64,128]{3,2,1,0:T(8,128)S(1)}, f32[2,4,64,128]{3,2,1,0:T(8,128)S(1)}) custom-call(s32[8]{0:T(128)S(4)} %get-tuple-element.21.widths, bf16[64,64]{1,0:T(8,128)(2,1)S(1)} %copy-done, f32[6,1536,128]{2,1,0:T(8,128)S(1)} %get-tuple-element.25.cells, f32[32,64,128]{2,1,0:T(8,128)S(1)} %get-tuple-element.22.weights, ...), custom_call_target="tpu_custom_call" | custom-call | flops 1000000000 | bytes 1000000 | tf_op jit(solution)/shard_map/pallas_call | solution.py:514
  16.2 0.0 collective-permute-done.3.far
  16.2 0.0 collective-permute-done.4.near
  16.2 1.1 %shard_map.88 = (bf16[2,64,24,128]{3,2,1,0:T(8,128)(2,1)}, f32[2,1536,128]{2,1,0:T(8,128)S(1)}) custom-call(s32[8]{0:T(128)S(4)} %get-tuple-element.21.widths, bf16[64,64]{1,0:T(8,128)(2,1)S(1)} %copy-done, f32[32,64,128]{2,1,0:T(8,128)S(1)} %get-tuple-element.22.weights, ...), custom_call_target="tpu_custom_call", output_to_operand_aliasing={{1}: (7, {})} | custom-call | tf_op jit(solution)/shard_map/pallas_call | solution.py:528
Async XLA Ops:
  3.0 5.2 %collective-permute-start = (bf16[80,128]{1,0:T(8,128)(2,1)S(1)}, bf16[80,128]{1,0:T(8,128)(2,1)S(1)}, u32[]{:S(2)}, u32[]{:S(2)}) collective-permute-start(bf16[80,128]{1,0:T(8,128)(2,1)S(1)} %get-tuple-element.26), channel_id=1, source_target_pairs={{0,1},{1,2},{2,3},{3,0},{4,5},{5,6},{6,7},{7,4},{8,9},{9,10},{10,1... | collective-permute-start | bytes 61448 | tf_op jit(solution)/shard_map/ppermute | solution.py:469
  5.0 3.1 %collective-permute-start.1 = (bf16[80,128]{1,0:T(8,128)(2,1)S(1)}, bf16[80,128]{1,0:T(8,128)(2,1)S(1)}, u32[]{:S(2)}, u32[]{:S(2)}) collective-permute-start(bf16[80,128]{1,0:T(8,128)(2,1)S(1)} %get-tuple-element.27), channel_id=1, source_target_pairs={{1,0},{2,1},{3,2},{0,3},{5,4},{6,5},{7,6},{4,7},{9,8},{10,9},{11,1... | collective-permute-start | bytes 61448 | tf_op jit(solution)/shard_map/ppermute | solution.py:470
  6.4 8.5 %collective-permute-start.2 = (f32[3,2,32]{2,1,0:T(2,128)S(1)}, f32[3,2,32]{2,1,0:T(2,128)S(1)}, u32[]{:S(2)}, u32[]{:S(2)}) collective-permute-start(f32[3,2,32]{2,1,0:T(2,128)S(1)} %get-tuple-element.30.refs_2_), channel_id=1, source_target_pairs={{0,2},{1,3},{2,0},{3,1},{4,6},{5,7},{6,4},{7,5},{8,10},{9,11},{10,... | collective-permute-start | bytes 2312 | tf_op jit(solution)/shard_map/ppermute | solution.py:485
  8.4 7.8 %collective-permute-start.3 = (bf16[256,128]{1,0:T(8,128)(2,1)S(1)}, bf16[256,128]{1,0:T(8,128)(2,1)S(1)}, u32[]{:S(2)}, u32[]{:S(2)}) collective-permute-start(bf16[256,128]{1,0:T(8,128)(2,1)S(1)} %get-tuple-element.33), channel_id=1, source_target_pairs={{4,8},{8,4},{12,16},{16,12},{20,24},{24,20},{28,0},{0,28},{5,9},{9... | collective-permute-start | bytes 196616 | tf_op jit(solution)/shard_map/ppermute | solution.py:426
  11.2 5.0 %collective-permute-start.4 = (bf16[256,128]{1,0:T(8,128)(2,1)S(1)}, bf16[256,128]{1,0:T(8,128)(2,1)S(1)}, u32[]{:S(2)}, u32[]{:S(2)}) collective-permute-start(bf16[256,128]{1,0:T(8,128)(2,1)S(1)} %get-tuple-element.34), channel_id=1, source_target_pairs={{0,4},{4,0},{8,12},{12,8},{16,20},{20,16},{24,28},{28,24},{1,5},{5... | collective-permute-start | bytes 196616 | tf_op jit(solution)/shard_map/ppermute | solution.py:426
  12.3 2.6 %copy-start = (bf16[64,64]{1,0:T(8,128)(2,1)S(1)}, bf16[64,64]{1,0:T(8,128)(2,1)}, u32[]{:S(2)}) copy-start(bf16[64,64]{1,0:T(8,128)(2,1)} %mix.3) | copy-start | bytes 24580

commit v2 on v1

--- a/solution.py
+++ b/solution.py
@@ -12,8 +12,8 @@
 CF = 16
 ROWS = 8
 SPLIT = 1
-CHUNK = 16
-DW_BIAS, PW_BIAS, LIFT = 27, 28, 29
+STORED = 32
+DW_BIAS, PW_BIAS, LIFT = 0, 1, 2
 F32 = jnp.float32
 BF16 = jnp.bfloat16
 VMEM_BYTES = 14 * 1024 * 1024
@@ -36,17 +36,15 @@
 
 
 def pack_kernel(
-    feature, widths_in, taps_in, dw_bias_in, pw_bias_in, lift_in, coarse_in,
+    feature, widths_in, taps_in, coarse_in,
     cells, weights, first, second, own_block, widths,
-    planes, widths_here, taps, dw_bias, pw_bias, lift, coarse, stacked, tail, picked, sems, small_sems,
+    planes, widths_here, taps, coarse, tail, picked, sems, small_sems,
 ):
     count, channels, slots, tile = feature.shape
 
-    half_of = channels // 2
-
-    def copy_of(m, part):
-        at = (pl.ds(ZOUT * m, ZOUT), pl.ds(part * half_of, half_of))
-        return pltpu.make_async_copy(feature.at[at], planes.at[at], sems.at[m, part])
+    def copy_of(m):
+        at = pl.ds(ZOUT * m, ZOUT)
+        return pltpu.make_async_copy(feature.at[at], planes.at[at], sems.at[m])
 
     small = [
         pltpu.make_async_copy(source, target, small_sems.at[i])
@@ -54,29 +52,22 @@
             (
                 (widths_in, widths_here),
                 (taps_in, taps),
-                (dw_bias_in, dw_bias),
-                (pw_bias_in, pw_bias),
-                (lift_in, lift),
                 (coarse_in, coarse),
             )
         )
     ]
+    copy_of(0).start()
     for copy in small:
         copy.start()
-    for m in range(3):
-        for part in range(2):
-            copy_of(m, part).start()
+    for m in range(1, 3):
+        copy_of(m).start()
     def take_small():
         for copy in small:
             copy.wait()
         for d in range(widths.shape[0]):
             widths[d] = widths_here[d]
-        stacked[0:DW_BIAS, :] = taps[...]
-        stacked[DW_BIAS : DW_BIAS + 1, :] = dw_bias[...]
-        stacked[PW_BIAS : PW_BIAS + 1, :] = pw_bias[...]
-        stacked[LIFT : LIFT + 3, :] = lift[...]
-        turned = jnp.transpose(stacked[...])
-        for t in range(stacked.shape[0]):
+        turned = jnp.transpose(taps[...])
+        for t in range(weights.shape[0]):
             weights[t] = jnp.broadcast_to(turned[:, t : t + 1], (channels, tile))
 
         own_block[...] = coarse[...]
@@ -124,11 +115,10 @@
         )
 
     for m in range(3):
-        for part in range(2):
-            copy_of(m, part).wait()
-            for c in range(part * half_of, (part + 1) * half_of, ROWS):
-                for half, total in enumerate(summed(m, c, ROWS // 2)):
-                    picked[m, half, c : c + ROWS, :] = total
+        copy_of(m).wait()
+        for c in range(0, channels, ROWS):
+            for half, total in enumerate(summed(m, c, ROWS // 2)):
+                picked[m, half, c : c + ROWS, :] = total
         if m == 0:
             take_small()
     width = widths_here[lax.axis_index("gx")]
@@ -191,11 +181,17 @@
                         depth[z, out, to, :] = shifted_sum(*(sums.pop((out, dy)) for dy in (-1, 0, 1)))
 
 
-def outer_kernel(widths, weights, coarse, cells_in, cells, rims, own_block):
+def outer_kernel(widths, weights, dw_bias, pw_bias, lift, coarse, cells_in, cells, extras, rims, own_block, stacked):
     width = widths[lax.axis_index("gx")]
     channels, tile = weights.shape[1:]
     slots = cells.shape[1] // channels
     own_block[...] = coarse[...]
+    stacked[DW_BIAS : DW_BIAS + 1, :] = dw_bias[...]
+    stacked[PW_BIAS : PW_BIAS + 1, :] = pw_bias[...]
+    stacked[LIFT : LIFT + 3, :] = lift[...]
+    turned = jnp.transpose(stacked[...])
+    for t in range(extras.shape[0]):
+        extras[t] = jnp.broadcast_to(turned[:, t : t + 1], (channels, tile))
     for b in range(channels // ROWS):
         at = slice(b * ROWS, (b + 1) * ROWS)
         for side, dx in enumerate((1, -1)):
@@ -271,9 +267,9 @@
     return start
 
 
-def depth_row(weights, depths, edge, z, x):
+def depth_row(extras, depths, edge, z, x):
     own = jnp.concatenate([depth[z, x] for depth in depths], axis=0)
-    return own + weights[DW_BIAS] + edge_term(edge, z, x)
+    return own + extras[DW_BIAS] + edge_term(edge, z, x)
 
 
 def base_row(cells, lifted, phase, z, x):
@@ -282,12 +278,12 @@
     return cells[2 + z, pl.ds(x, channels, stride=slots), :] + lifted[lax.div(phase + x, CF)]
 
 
-def active(weights, mixed):
-    mixed = mixed + weights[PW_BIAS]
+def active(extras, mixed):
+    mixed = mixed + extras[PW_BIAS]
     return jnp.maximum(mixed, 0.2 * mixed)
 
 
-def mix_kernel(gathered, widths, mix, cells, weights, depth, rest, edge, *refs):
+def mix_kernel(gathered, widths, mix, cells, extras, depth, rest, edge, *refs):
     if gathered:
         coarse, value, ends, bases, lifted, across, mixer = refs
         parts, ncx, ncy = coarse.shape
@@ -299,7 +295,7 @@
     here = lax.axis_index("gy")
     start = slab_start(widths)
     phase = lax.rem(start, CF)
-    channels, tile = weights.shape[1:]
+    channels, tile = extras.shape[1:]
     slots = cells.shape[1] // channels
 
     if not gathered:
@@ -323,7 +319,7 @@
         cell = lax.rem(lax.div(start, CF) + i, ncx)
         total = None
         for k in range(parts):
-            term = weights[LIFT + k] * across[k, pl.ds(cell, 1), :]
+            term = extras[LIFT + k] * across[k, pl.ds(cell, 1), :]
             total = term if total is None else total + term
         lifted[i] = total
 
@@ -341,14 +337,14 @@
     def mix_rows(begin, end):
         for x in range(begin, end, group):
             depths = [
-                jnp.concatenate([depth_row(weights, (depth, rest), edge, z, x + i) for i in range(group)], axis=0)
+                jnp.concatenate([depth_row(extras, (depth, rest), edge, z, x + i) for i in range(group)], axis=0)
                 for z in range(ZOUT)
             ]
             mixed = jnp.dot(mixer[...], jnp.concatenate(depths, axis=1).astype(BF16), preferred_element_type=F32)
             for i in range(group):
                 for z in range(ZOUT):
                     part = mixed[i * channels : (i + 1) * channels, z * tile : (z + 1) * tile]
-                    part = active(weights, part) + base_row(cells, lifted, phase, z, x + i)
+                    part = active(extras, part) + base_row(cells, lifted, phase, z, x + i)
                     if x + i >= end - ROWS and begin:
                         part = jnp.where(x + i < width, part, 0.0)
                     value[z, pl.ds(x + i, channels, stride=slots), :] = part
@@ -356,7 +352,7 @@
     mix_rows(0, ROWS)
     for z in range(ZOUT):
         for i, x in enumerate((0, 1, width - 2, width - 1)):
-            ends[z, i] = depth_row(weights, (depth, rest), edge, z, x)
+            ends[z, i] = depth_row(extras, (depth, rest), edge, z, x)
             bases[z, i] = base_row(cells, lifted, phase, z, x)
 
     def further_rows(limit):
@@ -369,9 +365,9 @@
         pl.when((width > limit - ROWS) & (width <= limit))(lambda limit=limit: further_rows(limit))
 
 
-def finish_kernel(widths, mix, weights, ends, bases, far, near, value_in, out, value, block, sems):
+def finish_kernel(widths, mix, extras, ends, bases, far, near, value_in, out, value, block, sems):
     width = widths[lax.axis_index("gx")]
-    channels, tile = weights.shape[1:]
+    channels, tile = extras.shape[1:]
     slots = block.shape[2]
     even = is_even("gx")
     mixed = []
@@ -385,15 +381,15 @@
         mixed.append(jnp.dot(mix[...], jnp.concatenate(sums, axis=1), preferred_element_type=F32))
     copies = []
     for z in range(ZOUT):
-        for part in range(channels // CHUNK):
-            at = slice(part * CHUNK, (part + 1) * CHUNK)
+        for part in range(channels // STORED):
+            at = slice(part * STORED, (part + 1) * STORED)
             for i, x in enumerate((0, 1, width - 2, width - 1)):
-                rows = mixed[z][at, i * tile : (i + 1) * tile] + weights[PW_BIAS, at, :]
+                rows = mixed[z][at, i * tile : (i + 1) * tile] + extras[PW_BIAS, at, :]
                 rows = jnp.maximum(rows, 0.2 * rows) + bases[z, i, at, :]
-                value[z, pl.ds(part * CHUNK * slots + x, CHUNK, stride=slots), :] = rows
-            for o in range(part * CHUNK, (part + 1) * CHUNK):
+                value[z, pl.ds(part * STORED * slots + x, STORED, stride=slots), :] = rows
+            for o in range(part * STORED, (part + 1) * STORED):
                 block[z, o] = value[z, o * slots : (o + 1) * slots, :].astype(BF16)
-            part_of = pl.ds(part * CHUNK, CHUNK)
+            part_of = pl.ds(part * STORED, STORED)
             copy = pltpu.make_async_copy(block.at[z, part_of], out.at[z, part_of], sems.at[part, z])
             copy.start()
             copies.append(copy)
@@ -430,57 +426,50 @@
 
     if gathered:
         every = lax.all_gather(coarse, "gy", axis=1, tiled=True)
-    small = (
-        widths,
-        dw_weight,
-        dw_bias.reshape(1, channels),
-        pw_bias.reshape(1, channels),
-        lift_weight.T,
-        coarse,
-    )
+    small = (widths, dw_weight, coarse)
     cells, weights, first, second, block, slab_widths = pl.pallas_call(
         pack_kernel,
         out_shape=(
             cells_shape,
-            pltpu.VMEM((32, channels, tile), F32),
+            pltpu.VMEM((27, channels, tile), F32),
             strip,
             strip,
             pltpu.VMEM(coarse.shape, F32),
             pltpu.SMEM(widths.shape, jnp.int32),
         ),
-        in_specs=[hbm] * 7,
+        in_specs=[hbm] * 4,
         out_specs=(vmem,) * 5 + (smem,),
         scratch_shapes=[
             pltpu.VMEM(feature.shape, BF16),
             pltpu.SMEM(widths.shape, jnp.int32),
             pltpu.VMEM(dw_weight.shape, F32),
-            pltpu.VMEM((1, channels), F32),
-            pltpu.VMEM((1, channels), F32),
-            pltpu.VMEM((parts, channels), F32),
             pltpu.VMEM(coarse.shape, F32),
-            pltpu.VMEM((32, channels), F32),
             pltpu.VMEM((16, tile), F32),
             pltpu.VMEM((3, 2, channels, tile), F32),
-            pltpu.SemaphoreType.DMA((3, 2)),
+            pltpu.SemaphoreType.DMA((3,)),
             pltpu.SemaphoreType.DMA((len(small),)),
         ],
         compiler_params=params,
     )(pinned(feature), *(pinned(array) for array in small))
     first = lax.ppermute(first, "gy", [(i, (i + 1) % ny) for i in range(ny)])
     second = lax.ppermute(second, "gy", [((i + 1) % ny, i) for i in range(ny)])
-    cells, rims, own_block = pl.pallas_call(
+    cells, extras, rims, own_block = pl.pallas_call(
         outer_kernel,
         out_shape=(
             cells_shape,
+            pltpu.VMEM((5, channels, tile), F32),
             pltpu.VMEM((ZOUT, 4, channels, tile), F32),
             pltpu.VMEM(coarse.shape, F32),
         ),
-        in_specs=[smem] + [vmem] * 3,
-        out_specs=(vmem,) * 3,
-        input_output_aliases={3: 0},
+        in_specs=[smem] + [vmem] * 6,
+        out_specs=(vmem,) * 4,
+        scratch_shapes=[pltpu.VMEM((8, channels), F32)],
+        input_output_aliases={6: 0},
         compiler_params=params,
         cost_estimate=pl.CostEstimate(flops=10**8, bytes_accessed=10**6, transcendentals=0),
-    )(slab_widths, weights, block, cells)
+    )(
+        slab_widths, weights, dw_bias.reshape(1, channels), pw_bias.reshape(1, channels), lift_weight.T, block, cells
+    )
     if not gathered:
         opposite = lax.ppermute(own_block, "gy", [(i, (i + 2) % 4) for i in range(4)])
     early = SPLIT * ROWS
@@ -524,7 +513,7 @@
         + ([] if gathered else [pltpu.VMEM((parts, ncx, ncy), F32)]),
         compiler_params=params,
         cost_estimate=pl.CostEstimate(flops=10**9, bytes_accessed=10**6, transcendentals=0),
-    )(slab_widths, pw_weight, cells, weights, depth, rest, edge, *blocks)
+    )(slab_widths, pw_weight, cells, extras, depth, rest, edge, *blocks)
     out, _ = pl.pallas_call(
         finish_kernel,
         out_shape=(shape((ZOUT, channels, slots, tile), BF16), value_shape),
@@ -532,11 +521,11 @@
         out_specs=(hbm, vmem),
         scratch_shapes=[
             pltpu.VMEM((ZOUT, channels, slots, tile), BF16),
-            pltpu.SemaphoreType.DMA((channels // CHUNK, ZOUT)),
+            pltpu.SemaphoreType.DMA((channels // STORED, ZOUT)),
         ],
         input_output_aliases={7: 1},
         compiler_params=params,
-    )(slab_widths, pw_weight, weights, ends, bases, far, near, value)
+    )(slab_widths, pw_weight, extras, ends, bases, far, near, value)
     return out
 
 

time: 17.5 us -> 16.9 us (0.966)
  the two profiles are of different devices: /device:TPU:1 before, /device:TPU:0 now
where the time goes in v2:
time: 16.9 us; the launch traced here: 16.8 us
  starting transfers between devices  8.36 us (49%)
  Pallas kernels  7.66 us (45%)
  waiting for transfers between devices  0.66 us (4%)
    ppermute x1, starting transfers between devices, shards(): first = lax.ppermute(first, 'gy', [(i, (i + 1) % ny) for i in range(ny)])  2.99 us
    pallas_call x1, Pallas kernels, shards(): pl.pallas_call(pack_kernel, out_shape=(cells_shape, pltpu.VMEM((27, chann...  2.75 us
    ppermute x2, starting transfers between devices, swapped(): return lax.ppermute(array, axis, pairs)  2.35 us
    ppermute x1, starting transfers between devices, shards(): lax.ppermute(own_block, 'gy', [(i, (i + 2) % 4) for i in range(4)])  2 us
    pallas_call x1, Pallas kernels, shards(): pl.pallas_call(rest_kernel, out_shape=pltpu.VMEM((ZOUT, slots, channels -...  1.72 us
    pallas_call x1, Pallas kernels, shards(): pl.pallas_call(functools.partial(mix_kernel, gathered), out_shape=(value_...  1.17 us
    pallas_call x1, Pallas kernels, shards(): pl.pallas_call(finish_kernel, out_shape=(shape((ZOUT, channels, slots, ti...  1.12 us
    ppermute x1, starting transfers between devices, shards(): second = lax.ppermute(second, 'gy', [((i + 1) % ny, i) for i in range(ny)])  1.02 us
  transfers between devices with their start and end apart: 5, of which 1 were waited for; matrix products, arithmetic and copies ran while one was open for 0% of the time, Pallas kernels for 23%

profile of v2, /device:TPU:0, one launch (start us, length us, event | category | flops | bytes accessed | tf_op | source)
XLA Modules:
  0.0 16.8 jit_solution(13624063650888591198)
XLA Ops:
  0.0 0.0 copy-start.1
  0.0 0.0 copy-start.3
  0.0 0.0 copy-start.2
  0.0 2.7 %shard_map.82 = (f32[6,1536,128]{2,1,0:T(8,128)S(1)}, f32[27,64,128]{2,1,0:T(8,128)S(1)}, bf16[80,128]{1,0:T(8,128)(2,1)S(1)}, bf16[80,128]{1,0:T(8,128)(2,1)S(1...) custom-call(bf16[6,64,24,128]{3,2,1,0:T(8,128)(2,1)} %feature.1, s32[8]{0:T(128)} %widths_in.1, f32[27,64]{1,0:T(8,128)} %taps_in.1, ...), custom_call_target="tpu_custom_call" | custom-call | tf_op jit(solution)/shard_map/pallas_call | solution.py:430
  2.8 3.0 %collective-permute-start = (bf16[80,128]{1,0:T(8,128)(2,1)S(1)}, bf16[80,128]{1,0:T(8,128)(2,1)S(1)}, u32[]{:S(2)}, u32[]{:S(2)}) collective-permute-start(bf16[80,128]{1,0:T(8,128)(2,1)S(1)} %get-tuple-element.28), channel_id=1, source_target_pairs={{0,1},{1,2},{2,3},{3,0},{4,5},{5,6},{6,7},{7,4},{8,9},{9,10},{10,1... | collective-permute-start | bytes 61448 | tf_op jit(solution)/shard_map/ppermute | solution.py:454
  5.8 1.0 %collective-permute-start.1 = (bf16[80,128]{1,0:T(8,128)(2,1)S(1)}, bf16[80,128]{1,0:T(8,128)(2,1)S(1)}, u32[]{:S(2)}, u32[]{:S(2)}) collective-permute-start(bf16[80,128]{1,0:T(8,128)(2,1)S(1)} %get-tuple-element.29), channel_id=1, source_target_pairs={{1,0},{2,1},{3,2},{0,3},{5,4},{6,5},{7,6},{4,7},{9,8},{10,9},{11,1... | collective-permute-start | bytes 61448 | tf_op jit(solution)/shard_map/ppermute | solution.py:455
  6.8 0.0 copy-done.1
  6.8 0.0 copy-done.3
  6.8 0.0 copy-done.2
  6.8 0.5 %shard_map.83 = (f32[6,1536,128]{2,1,0:T(8,128)S(1)}, f32[5,64,128]{2,1,0:T(8,128)S(1)}, f32[2,4,64,128]{3,2,1,0:T(8,128)S(1)}, f32[3,2,32]{2,1,0:T(2,128)S(1)}) custom-call(s32[8]{0:T(128)S(4)} %get-tuple-element.22.widths, f32[27,64,128]{2,1,0:T(8,128)S(1)} %get-tuple-element.23.weights, f32[1,64]{1,0:T(1,128)S(1)} %bitcast.4, ...), custom_call_target="tpu_custom_call", output_to_operand_aliasing={{0}: (6, {})} | custom-call | flops 100000000 | bytes 1000000 | tf_op jit(solution)/shard_map/pallas_call | solution.py:456
  7.3 2.0 %collective-permute-start.2 = (f32[3,2,32]{2,1,0:T(2,128)S(1)}, f32[3,2,32]{2,1,0:T(2,128)S(1)}, u32[]{:S(2)}, u32[]{:S(2)}) collective-permute-start(f32[3,2,32]{2,1,0:T(2,128)S(1)} %get-tuple-element.32.refs_2_), channel_id=1, source_target_pairs={{0,2},{1,3},{2,0},{3,1},{4,6},{5,7},{6,4},{7,5},{8,10},{9,11},{10,... | collective-permute-start | bytes 2312 | tf_op jit(solution)/shard_map/ppermute | solution.py:474
  9.3 0.2 %shard_map.84.depth = f32[2,24,8,128]{3,2,1,0:T(8,128)S(1)} custom-call(s32[8]{0:T(128)S(4)} %get-tuple-element.22.widths, f32[6,1536,128]{2,1,0:T(8,128)S(1)} %get-tuple-element.27.cells, f32[27,64,128]{2,1,0:T(8,128)S(1)} %get-tuple-element.23.weights), custom_call_target="tpu_custom_call" | custom-call | flops 1000000000 | bytes 1000000 | tf_op jit(solution)/shard_map/pallas_call | solution.py:476
  9.5 0.0 collective-permute-done.first.refs_0_
  9.5 0.0 collective-permute-done.1.second.refs_1_
  9.5 0.2 %shard_map.85 = (f32[2,64,128]{2,1,0:T(8,128)S(1)}, bf16[256,128]{1,0:T(8,128)(2,1)S(1)}, bf16[256,128]{1,0:T(8,128)(2,1)S(1)}) custom-call(s32[8]{0:T(128)S(4)} %get-tuple-element.22.widths, bf16[80,128]{1,0:T(8,128)(2,1)S(1)} %collective-permute-done.first.refs_0_, bf16[80,128]{1,0:T(8,128)(2,1)S(1)} %collective-permute-done.1.second.refs_1_, ...), custom_call_target="tpu_custom_call" | custom-call | tf_op jit(solution)/shard_map/pallas_call | solution.py:484
  9.7 2.4 %collective-permute-start.3 = (bf16[256,128]{1,0:T(8,128)(2,1)S(1)}, bf16[256,128]{1,0:T(8,128)(2,1)S(1)}, u32[]{:S(2)}, u32[]{:S(2)}) collective-permute-start(bf16[256,128]{1,0:T(8,128)(2,1)S(1)} %get-tuple-element.35), channel_id=1, source_target_pairs={{4,8},{8,4},{12,16},{16,12},{20,24},{24,20},{28,0},{0,28},{5,9},{9... | collective-permute-start | bytes 196616 | tf_op jit(solution)/shard_map/ppermute | solution.py:422
  12.1 0.0 collective-permute-start.4
  12.1 0.0 copy-start
  12.1 1.7 %shard_map.86.rest = f32[2,24,56,128]{3,2,1,0:T(8,128)S(1)} custom-call(s32[8]{0:T(128)S(4)} %get-tuple-element.22.widths, f32[2,64,128]{2,1,0:T(8,128)S(1)} %get-tuple-element.31.edge, f32[6,1536,128]{2,1,0:T(8,128)S(1)} %get-tuple-element.27.cells, f32[27,64,128]{2,1,0:T(8,128)S(1)} %get-tuple-element.23.weights), custom_call_target="tpu_custom_call" | custom-call | flops 1000000000 | bytes 1000000 | tf_op jit(solution)/shard_map/pallas_call | solution.py:494
  13.8 0.0 collective-permute-done.2.refs_3_
  13.8 0.0 copy-done
  13.8 1.2 %shard_map.87 = (f32[2,1536,128]{2,1,0:T(8,128)S(1)}, f32[2,4,64,128]{3,2,1,0:T(8,128)S(1)}, f32[2,4,64,128]{3,2,1,0:T(8,128)S(1)}) custom-call(s32[8]{0:T(128)S(4)} %get-tuple-element.22.widths, bf16[64,64]{1,0:T(8,128)(2,1)S(1)} %copy-done, f32[6,1536,128]{2,1,0:T(8,128)S(1)} %get-tuple-element.27.cells, f32[5,64,128]{2,1,0:T(8,128)S(1)} %get-tuple-element.26.extras, ...), custom_call_target="tpu_custom_call" | custom-call | flops 1000000000 | bytes 1000000 | tf_op jit(solution)/shard_map/pallas_call | solution.py:503
  15.0 0.6 %collective-permute-done.3.far = bf16[256,128]{1,0:T(8,128)(2,1)S(1)} collective-permute-done((bf16[256,128]{1,0:T(8,128)(2,1)S(1)}, bf16[256,128]{1,0:T(8,128)(2,1)S(1)}, u32[]{:S(2)}, u32[]{:S(2)}) %collective-permute-start.3) | collective-permute-done | bytes 65568 | tf_op jit(solution)/shard_map/ppermute | solution.py:422
  15.6 0.0 collective-permute-done.4.near
  15.7 1.1 %shard_map.88 = (bf16[2,64,24,128]{3,2,1,0:T(8,128)(2,1)}, f32[2,1536,128]{2,1,0:T(8,128)S(1)}) custom-call(s32[8]{0:T(128)S(4)} %get-tuple-element.22.widths, bf16[64,64]{1,0:T(8,128)(2,1)S(1)} %copy-done, f32[5,64,128]{2,1,0:T(8,128)S(1)} %get-tuple-element.26.extras, ...), custom_call_target="tpu_custom_call", output_to_operand_aliasing={{1}: (7, {})} | custom-call | tf_op jit(solution)/shard_map/pallas_call | solution.py:517
Async XLA Ops:
  0.0 6.8 %copy-start.1 = (f32[64,3]{0,1:T(4,128)S(1)}, f32[64,3]{0,1:T(4,128)}, u32[]{:S(2)}) copy-start(f32[64,3]{0,1:T(4,128)} %param.14) | copy-start | bytes 2308
  0.0 6.8 %copy-start.3 = (f32[64]{0:T(128)S(1)}, f32[64]{0:T(128)}, u32[]{:S(2)}) copy-start(f32[64]{0:T(128)} %param.13) | copy-start | bytes 772
  0.0 6.8 %copy-start.2 = (f32[64]{0:T(128)S(1)}, f32[64]{0:T(128)}, u32[]{:S(2)}) copy-start(f32[64]{0:T(128)} %param.11) | copy-start | bytes 772
  2.8 6.8 %collective-permute-start = (bf16[80,128]{1,0:T(8,128)(2,1)S(1)}, bf16[80,128]{1,0:T(8,128)(2,1)S(1)}, u32[]{:S(2)}, u32[]{:S(2)}) collective-permute-start(bf16[80,128]{1,0:T(8,128)(2,1)S(1)} %get-tuple-element.28), channel_id=1, source_target_pairs={{0,1},{1,2},{2,3},{3,0},{4,5},{5,6},{6,7},{7,4},{8,9},{9,10},{10,1... | collective-permute-start | bytes 61448 | tf_op jit(solution)/shard_map/ppermute | solution.py:454
  5.8 3.8 %collective-permute-start.1 = (bf16[80,128]{1,0:T(8,128)(2,1)S(1)}, bf16[80,128]{1,0:T(8,128)(2,1)S(1)}, u32[]{:S(2)}, u32[]{:S(2)}) collective-permute-start(bf16[80,128]{1,0:T(8,128)(2,1)S(1)} %get-tuple-element.29), channel_id=1, source_target_pairs={{1,0},{2,1},{3,2},{0,3},{5,4},{6,5},{7,6},{4,7},{9,8},{10,9},{11,1... | collective-permute-start | bytes 61448 | tf_op jit(solution)/shard_map/ppermute | solution.py:455
  7.3 6.6 %collective-permute-start.2 = (f32[3,2,32]{2,1,0:T(2,128)S(1)}, f32[3,2,32]{2,1,0:T(2,128)S(1)}, u32[]{:S(2)}, u32[]{:S(2)}) collective-permute-start(f32[3,2,32]{2,1,0:T(2,128)S(1)} %get-tuple-element.32.refs_2_), channel_id=1, source_target_pairs={{0,2},{1,3},{2,0},{3,1},{4,6},{5,7},{6,4},{7,5},{8,10},{9,11},{10,... | collective-permute-start | bytes 2312 | tf_op jit(solution)/shard_map/ppermute | solution.py:474
  9.7 5.9 %collective-permute-start.3 = (bf16[256,128]{1,0:T(8,128)(2,1)S(1)}, bf16[256,128]{1,0:T(8,128)(2,1)S(1)}, u32[]{:S(2)}, u32[]{:S(2)}) collective-permute-start(bf16[256,128]{1,0:T(8,128)(2,1)S(1)} %get-tuple-element.35), channel_id=1, source_target_pairs={{4,8},{8,4},{12,16},{16,12},{20,24},{24,20},{28,0},{0,28},{5,9},{9... | collective-permute-start | bytes 196616 | tf_op jit(solution)/shard_map/ppermute | solution.py:422
  12.1 3.6 %collective-permute-start.4 = (bf16[256,128]{1,0:T(8,128)(2,1)S(1)}, bf16[256,128]{1,0:T(8,128)(2,1)S(1)}, u32[]{:S(2)}, u32[]{:S(2)}) collective-permute-start(bf16[256,128]{1,0:T(8,128)(2,1)S(1)} %get-tuple-element.36), channel_id=1, source_target_pairs={{0,4},{4,0},{8,12},{12,8},{16,20},{20,16},{24,28},{28,24},{1,5},{5... | collective-permute-start | bytes 196616 | tf_op jit(solution)/shard_map/ppermute | solution.py:422
  12.1 1.7 %copy-start = (bf16[64,64]{1,0:T(8,128)(2,1)S(1)}, bf16[64,64]{1,0:T(8,128)(2,1)}, u32[]{:S(2)}) copy-start(bf16[64,64]{1,0:T(8,128)(2,1)} %mix.3) | copy-start | bytes 24580

commit v3 on v2

--- a/solution.py
+++ b/solution.py
@@ -11,7 +11,7 @@
 ZOUT = 2
 CF = 16
 ROWS = 8
-SPLIT = 1
+EARLY, EARLY_WIDE = 1, 3
 STORED = 32
 DW_BIAS, PW_BIAS, LIFT = 0, 1, 2
 F32 = jnp.float32
@@ -85,30 +85,28 @@
 
     lane, row = lane_iota((slots, tile)), row_iota((slots, tile))
     mine = (lane >> 3) == (row & 15)
-    in_even, in_odd = mine & ((lane & 4) == 0), mine & ((lane & 4) != 0)
+    lane = lane_iota((ROWS * slots, tile))
+    of_second = (lane >= 2) & (lane < 6)
     sublane = row_iota((ROWS, tile))
 
-    def placed(m, k):
-        both = []
+    def merged(m, c):
+        rows = [planes[ZOUT * m + z, c : c + ROWS].reshape(ROWS * slots, tile) for z in range(ZOUT)]
         for z in range(ZOUT):
-            plane = planes[ZOUT * m + z, k].astype(F32)
-            cells[ZOUT * m + z, k * slots : (k + 1) * slots, :] = plane
-            both.append(
-                jnp.concatenate(
-                    [
-                        pltpu.roll(plane[x : x + ROWS], (2 + 4 * z + 8 * x) % tile, 1, stride=8, stride_axis=0)
-                        for x in range(0, slots, ROWS)
-                    ],
-                    axis=0,
-                )
+            cells[ZOUT * m + z, c * slots : (c + ROWS) * slots, :] = rows[z].astype(F32)
+        return jnp.where(of_second, pltpu.roll(rows[1], 4, 1), rows[0]).astype(F32)
+
+    def summed(rows, step):
+        if step == 0:
+            placed = jnp.concatenate(
+                [
+                    pltpu.roll(rows[x : x + ROWS], (2 + 8 * x) % tile, 1, stride=8, stride_axis=0)
+                    for x in range(0, slots, ROWS)
+                ],
+                axis=0,
             )
-        rows = jnp.where(in_even, both[0], jnp.where(in_odd, both[1], 0.0))
-        return rows[0:ROWS] + rows[ROWS : 2 * ROWS], rows[2 * ROWS :]
-
-    def summed(m, k, step):
-        if step == 0:
-            return placed(m, k)
-        one, two = summed(m, k, step // 2), summed(m, k + step, step // 2)
+            placed = jnp.where(mine, placed, 0.0)
+            return placed[0:ROWS] + placed[ROWS : 2 * ROWS], placed[2 * ROWS :]
+        one, two = summed(rows[: step * slots], step // 2), summed(rows[step * slots :], step // 2)
         turn = (sublane & step) != 0
         return tuple(
             jnp.where(turn, b, a) + pltpu.roll(jnp.where(turn, a, b), step, 0) for a, b in zip(one, two)
@@ -117,7 +115,7 @@
     for m in range(3):
         copy_of(m).wait()
         for c in range(0, channels, ROWS):
-            for half, total in enumerate(summed(m, c, ROWS // 2)):
+            for half, total in enumerate(summed(merged(m, c), ROWS // 2)):
                 picked[m, half, c : c + ROWS, :] = total
         if m == 0:
             take_small()
@@ -157,11 +155,10 @@
     return centre + before + after
 
 
-def convolve_block(cells, weights, depth, b, first, limit):
+def convolve_block(cells, weights, depth, b, limit):
     channels = weights.shape[1]
     slots = cells.shape[1] // channels
     at = pl.ds(pl.multiple_of(b * ROWS, ROWS), ROWS)
-    to = pl.ds(pl.multiple_of((b - first) * ROWS, ROWS), ROWS)
     tap = [weights[t, at, :] for t in range(27)]
     for z in range(ZOUT):
         for parity in range(2):
@@ -178,7 +175,7 @@
                                 sums[key] = sums[key] + term if key in sums else term
                 for out in [x - 2] if x + 2 < limit else [x - 2, x]:
                     if out >= 0:
-                        depth[z, out, to, :] = shifted_sum(*(sums.pop((out, dy)) for dy in (-1, 0, 1)))
+                        depth[z, out, at, :] = shifted_sum(*(sums.pop((out, dy)) for dy in (-1, 0, 1)))
 
 
 def outer_kernel(widths, weights, dw_bias, pw_bias, lift, coarse, cells_in, cells, extras, rims, own_block, stacked):
@@ -220,18 +217,26 @@
         @pl.when((width > limit - ROWS) & (width <= limit))
         def _():
             def convolve(b, carry):
-                convolve_block(cells, weights, depth, b, first, limit)
+                convolve_block(cells, weights, depth, b, limit)
                 return carry
 
             lax.fori_loop(first, last, convolve, 0)
 
 
+def early_blocks(widths, slots):
+    wide = widths[lax.axis_index("gx")] > slots - ROWS
+    return jnp.where(wide & jnp.logical_not(is_even("gx")), EARLY_WIDE, EARLY)
+
+
 def early_kernel(widths, cells, weights, depth):
-    convolve_blocks(widths, cells, weights, depth, 0, SPLIT)
-
-
-def rest_kernel(widths, edge, cells, weights, depth):
-    convolve_blocks(widths, cells, weights, depth, SPLIT, weights.shape[1] // ROWS)
+    slots = cells.shape[1] // weights.shape[1]
+    convolve_blocks(widths, cells, weights, depth, 0, early_blocks(widths, slots))
+
+
+def rest_kernel(widths, edge, cells, weights, depth_in, depth):
+    channels = weights.shape[1]
+    first = early_blocks(widths, cells.shape[1] // channels)
+    convolve_blocks(widths, cells, weights, depth, first, channels // ROWS)
 
 
 def edge_term(edge, z, x):
@@ -267,9 +272,8 @@
     return start
 
 
-def depth_row(extras, depths, edge, z, x):
-    own = jnp.concatenate([depth[z, x] for depth in depths], axis=0)
-    return own + extras[DW_BIAS] + edge_term(edge, z, x)
+def depth_row(extras, depth, edge, z, x):
+    return depth[z, x] + extras[DW_BIAS] + edge_term(edge, z, x)
 
 
 def base_row(cells, lifted, phase, z, x):
@@ -283,7 +287,7 @@
     return jnp.maximum(mixed, 0.2 * mixed)
 
 
-def mix_kernel(gathered, widths, mix, cells, extras, depth, rest, edge, *refs):
+def mix_kernel(gathered, widths, mix, cells, extras, depth, edge, *refs):
     if gathered:
         coarse, value, ends, bases, lifted, across, mixer = refs
         parts, ncx, ncy = coarse.shape
@@ -337,7 +341,7 @@
     def mix_rows(begin, end):
         for x in range(begin, end, group):
             depths = [
-                jnp.concatenate([depth_row(extras, (depth, rest), edge, z, x + i) for i in range(group)], axis=0)
+                jnp.concatenate([depth_row(extras, depth, edge, z, x + i) for i in range(group)], axis=0)
                 for z in range(ZOUT)
             ]
             mixed = jnp.dot(mixer[...], jnp.concatenate(depths, axis=1).astype(BF16), preferred_element_type=F32)
@@ -352,7 +356,7 @@
     mix_rows(0, ROWS)
     for z in range(ZOUT):
         for i, x in enumerate((0, 1, width - 2, width - 1)):
-            ends[z, i] = depth_row(extras, (depth, rest), edge, z, x)
+            ends[z, i] = depth_row(extras, depth, edge, z, x)
             bases[z, i] = base_row(cells, lifted, phase, z, x)
 
     def further_rows(limit):
@@ -472,10 +476,10 @@
     )
     if not gathered:
         opposite = lax.ppermute(own_block, "gy", [(i, (i + 2) % 4) for i in range(4)])
-    early = SPLIT * ROWS
+    depth_shape = pltpu.VMEM((ZOUT, slots, channels, tile), F32)
     depth = pl.pallas_call(
         early_kernel,
-        out_shape=pltpu.VMEM((ZOUT, slots, early, tile), F32),
+        out_shape=depth_shape,
         in_specs=[smem] + [vmem] * 2,
         out_specs=vmem,
         compiler_params=params,
@@ -491,19 +495,20 @@
     far = swapped(far, "gx", 1)
     near = swapped(near, "gx", 0)
     blocks = (every,) if gathered else (first, second, own_block, opposite)
-    rest = pl.pallas_call(
+    depth = pl.pallas_call(
         rest_kernel,
-        out_shape=pltpu.VMEM((ZOUT, slots, channels - early, tile), F32),
-        in_specs=[smem] + [vmem] * 3,
+        out_shape=depth_shape,
+        in_specs=[smem] + [vmem] * 4,
         out_specs=vmem,
+        input_output_aliases={4: 0},
         compiler_params=params,
         cost_estimate=pl.CostEstimate(flops=10**9, bytes_accessed=10**6, transcendentals=0),
-    )(slab_widths, edge, cells, weights)
+    )(slab_widths, edge, cells, weights, depth)
     ends_shape = pltpu.VMEM((ZOUT, 4, channels, tile), F32)
     value, ends, bases = pl.pallas_call(
         functools.partial(mix_kernel, gathered),
         out_shape=(value_shape, ends_shape, ends_shape),
-        in_specs=[smem] + [vmem] * (6 + len(blocks)),
+        in_specs=[smem] + [vmem] * (5 + len(blocks)),
         out_specs=(vmem,) * 3,
         scratch_shapes=[
             pltpu.VMEM((3, channels, tile), F32),
@@ -513,7 +518,7 @@
         + ([] if gathered else [pltpu.VMEM((parts, ncx, ncy), F32)]),
         compiler_params=params,
         cost_estimate=pl.CostEstimate(flops=10**9, bytes_accessed=10**6, transcendentals=0),
-    )(slab_widths, pw_weight, cells, extras, depth, rest, edge, *blocks)
+    )(slab_widths, pw_weight, cells, extras, depth, edge, *blocks)
     out, _ = pl.pallas_call(
         finish_kernel,
         out_shape=(shape((ZOUT, channels, slots, tile), BF16), value_shape),

time: 16.9 us -> 18 us (1.065)
  Pallas kernels: 7.66 us -> 8.54 us
  starting transfers between devices: 8.36 us -> 9.06 us
  waiting for transfers between devices: 0.66 us -> 0.01 us
    pallas_call x1, Pallas kernels: 2.75 us -> 3.56 us  [shards(): pl.pallas_call(pack_kernel, out_shape=(cells_shape, pltpu.VMEM((27, chann...]
    ppermute x2, starting transfers between devices: 2.35 us -> 3.06 us  [swapped(): return lax.ppermute(array, axis, pairs)]
    ppermute x2, waiting for transfers between devices: 0.64 us -> 0.01 us  [swapped(): return lax.ppermute(array, axis, pairs)]
  transfers between devices with their start and end apart: 5 -> 5, of which waited for: 1 -> 0; matrix products, arithmetic and copies ran while one was open for 0% -> 0% of each run, Pallas kernels for 23% -> 22%
where the time goes in v3:
time: 18 us; the launch traced here: 17.7 us
  starting transfers between devices  9.06 us (50%)
  Pallas kernels  8.54 us (47%)
    pallas_call x1, Pallas kernels, shards(): pl.pallas_call(pack_kernel, out_shape=(cells_shape, pltpu.VMEM((27, chann...  3.56 us
    ppermute x2, starting transfers between devices, swapped(): return lax.ppermute(array, axis, pairs)  3.06 us
    ppermute x1, starting transfers between devices, shards(): first = lax.ppermute(first, 'gy', [(i, (i + 1) % ny) for i in range(ny)])  2.99 us
    ppermute x1, starting transfers between devices, shards(): lax.ppermute(own_block, 'gy', [(i, (i + 2) % 4) for i in range(4)])  2 us
    pallas_call x1, Pallas kernels, shards(): pl.pallas_call(rest_kernel, out_shape=depth_shape, in_specs=[smem] + [vme...  1.73 us
    pallas_call x1, Pallas kernels, shards(): pl.pallas_call(functools.partial(mix_kernel, gathered), out_shape=(value_...  1.18 us
    pallas_call x1, Pallas kernels, shards(): pl.pallas_call(finish_kernel, out_shape=(shape((ZOUT, channels, slots, ti...  1.14 us
    ppermute x1, starting transfers between devices, shards(): second = lax.ppermute(second, 'gy', [((i + 1) % ny, i) for i in range(ny)])  1.02 us
  transfers between devices with their start and end apart: 5, of which 0 were waited for; matrix products, arithmetic and copies ran while one was open for 0% of the time, Pallas kernels for 22%

profile of v3, /device:TPU:0, one launch (start us, length us, event | category | flops | bytes accessed | tf_op | source)
XLA Modules:
  0.0 17.7 jit_solution(9145975638418337902)
XLA Ops:
  0.0 0.0 copy-start.1
  0.0 0.0 copy-start.3
  0.0 0.0 copy-start.2
  0.0 3.6 %shard_map.82 = (f32[6,1536,128]{2,1,0:T(8,128)S(1)}, f32[27,64,128]{2,1,0:T(8,128)S(1)}, bf16[80,128]{1,0:T(8,128)(2,1)S(1)}, bf16[80,128]{1,0:T(8,128)(2,1)S(1...) custom-call(bf16[6,64,24,128]{3,2,1,0:T(8,128)(2,1)} %feature.1, s32[8]{0:T(128)} %widths_in.1, f32[27,64]{1,0:T(8,128)} %taps_in.1, ...), custom_call_target="tpu_custom_call" | custom-call | tf_op jit(solution)/shard_map/pallas_call | solution.py:434
  3.6 3.0 %collective-permute-start = (bf16[80,128]{1,0:T(8,128)(2,1)S(1)}, bf16[80,128]{1,0:T(8,128)(2,1)S(1)}, u32[]{:S(2)}, u32[]{:S(2)}) collective-permute-start(bf16[80,128]{1,0:T(8,128)(2,1)S(1)} %get-tuple-element.28), channel_id=1, source_target_pairs={{0,1},{1,2},{2,3},{3,0},{4,5},{5,6},{6,7},{7,4},{8,9},{9,10},{10,1... | collective-permute-start | bytes 61448 | tf_op jit(solution)/shard_map/ppermute | solution.py:458
  6.6 1.0 %collective-permute-start.1 = (bf16[80,128]{1,0:T(8,128)(2,1)S(1)}, bf16[80,128]{1,0:T(8,128)(2,1)S(1)}, u32[]{:S(2)}, u32[]{:S(2)}) collective-permute-start(bf16[80,128]{1,0:T(8,128)(2,1)S(1)} %get-tuple-element.29), channel_id=1, source_target_pairs={{1,0},{2,1},{3,2},{0,3},{5,4},{6,5},{7,6},{4,7},{9,8},{10,9},{11,1... | collective-permute-start | bytes 61448 | tf_op jit(solution)/shard_map/ppermute | solution.py:459
  7.6 0.0 copy-done.1
  7.6 0.0 copy-done.3
  7.6 0.0 copy-done.2
  7.6 0.5 %shard_map.83 = (f32[6,1536,128]{2,1,0:T(8,128)S(1)}, f32[5,64,128]{2,1,0:T(8,128)S(1)}, f32[2,4,64,128]{3,2,1,0:T(8,128)S(1)}, f32[3,2,32]{2,1,0:T(2,128)S(1)}) custom-call(s32[8]{0:T(128)S(4)} %get-tuple-element.22.widths, f32[27,64,128]{2,1,0:T(8,128)S(1)} %get-tuple-element.23.weights, f32[1,64]{1,0:T(1,128)S(1)} %bitcast.4, ...), custom_call_target="tpu_custom_call", output_to_operand_aliasing={{0}: (6, {})} | custom-call | flops 100000000 | bytes 1000000 | tf_op jit(solution)/shard_map/pallas_call | solution.py:460
  8.1 2.0 %collective-permute-start.2 = (f32[3,2,32]{2,1,0:T(2,128)S(1)}, f32[3,2,32]{2,1,0:T(2,128)S(1)}, u32[]{:S(2)}, u32[]{:S(2)}) collective-permute-start(f32[3,2,32]{2,1,0:T(2,128)S(1)} %get-tuple-element.32.refs_2_), channel_id=1, source_target_pairs={{0,2},{1,3},{2,0},{3,1},{4,6},{5,7},{6,4},{7,5},{8,10},{9,11},{10,... | collective-permute-start | bytes 2312 | tf_op jit(solution)/shard_map/ppermute | solution.py:478
  10.1 0.2 %shard_map.85.depth_in = f32[2,24,64,128]{3,2,1,0:T(8,128)S(1)} custom-call(s32[8]{0:T(128)S(4)} %get-tuple-element.22.widths, f32[6,1536,128]{2,1,0:T(8,128)S(1)} %get-tuple-element.27.cells, f32[27,64,128]{2,1,0:T(8,128)S(1)} %get-tuple-element.23.weights), custom_call_target="tpu_custom_call" | custom-call | flops 1000000000 | bytes 1000000 | tf_op jit(solution)/shard_map/pallas_call | solution.py:480
  10.4 0.0 collective-permute-done.first.refs_0_
  10.4 0.0 collective-permute-done.1.second.refs_1_
  10.4 0.2 %shard_map.84 = (f32[2,64,128]{2,1,0:T(8,128)S(1)}, bf16[256,128]{1,0:T(8,128)(2,1)S(1)}, bf16[256,128]{1,0:T(8,128)(2,1)S(1)}) custom-call(s32[8]{0:T(128)S(4)} %get-tuple-element.22.widths, bf16[80,128]{1,0:T(8,128)(2,1)S(1)} %collective-permute-done.first.refs_0_, bf16[80,128]{1,0:T(8,128)(2,1)S(1)} %collective-permute-done.1.second.refs_1_, ...), custom_call_target="tpu_custom_call" | custom-call | tf_op jit(solution)/shard_map/pallas_call | solution.py:488
  10.6 3.1 %collective-permute-start.3 = (bf16[256,128]{1,0:T(8,128)(2,1)S(1)}, bf16[256,128]{1,0:T(8,128)(2,1)S(1)}, u32[]{:S(2)}, u32[]{:S(2)}) collective-permute-start(bf16[256,128]{1,0:T(8,128)(2,1)S(1)} %get-tuple-element.35), channel_id=1, source_target_pairs={{4,8},{8,4},{12,16},{16,12},{20,24},{24,20},{28,0},{0,28},{5,9},{9... | collective-permute-start | bytes 196616 | tf_op jit(solution)/shard_map/ppermute | solution.py:426
  13.6 0.0 collective-permute-start.4
  13.6 0.0 copy-start
  13.6 1.7 %shard_map.86.depth = f32[2,24,64,128]{3,2,1,0:T(8,128)S(1)} custom-call(s32[8]{0:T(128)S(4)} %get-tuple-element.22.widths, f32[2,64,128]{2,1,0:T(8,128)S(1)} %get-tuple-element.31.edge, f32[6,1536,128]{2,1,0:T(8,128)S(1)} %get-tuple-element.27.cells, f32[27,64,128]{2,1,0:T(8,128)S(1)} %get-tuple-element.23.weights, ...), custom_call_target="tpu_custom_call", output_to_operand_aliasing={{}: (4, {})} | custom-call | flops 1000000000 | bytes 1000000 | tf_op jit(solution)/shard_map/pallas_call | solution.py:498
  15.4 0.0 collective-permute-done.2.refs_3_
  15.4 0.0 copy-done
  15.4 1.2 %shard_map.87 = (f32[2,1536,128]{2,1,0:T(8,128)S(1)}, f32[2,4,64,128]{3,2,1,0:T(8,128)S(1)}, f32[2,4,64,128]{3,2,1,0:T(8,128)S(1)}) custom-call(s32[8]{0:T(128)S(4)} %get-tuple-element.22.widths, bf16[64,64]{1,0:T(8,128)(2,1)S(1)} %copy-done, f32[6,1536,128]{2,1,0:T(8,128)S(1)} %get-tuple-element.27.cells, f32[5,64,128]{2,1,0:T(8,128)S(1)} %get-tuple-element.26.extras, ...), custom_call_target="tpu_custom_call" | custom-call | flops 1000000000 | bytes 1000000 | tf_op jit(solution)/shard_map/pallas_call | solution.py:508
  16.6 0.0 collective-permute-done.3.far
  16.6 0.0 collective-permute-done.4.near
  16.6 1.1 %shard_map.88 = (bf16[2,64,24,128]{3,2,1,0:T(8,128)(2,1)}, f32[2,1536,128]{2,1,0:T(8,128)S(1)}) custom-call(s32[8]{0:T(128)S(4)} %get-tuple-element.22.widths, bf16[64,64]{1,0:T(8,128)(2,1)S(1)} %copy-done, f32[5,64,128]{2,1,0:T(8,128)S(1)} %get-tuple-element.26.extras, ...), custom_call_target="tpu_custom_call", output_to_operand_aliasing={{1}: (7, {})} | custom-call | tf_op jit(solution)/shard_map/pallas_call | solution.py:522
Async XLA Ops:
  0.0 7.6 %copy-start.1 = (f32[64,3]{0,1:T(4,128)S(1)}, f32[64,3]{0,1:T(4,128)}, u32[]{:S(2)}) copy-start(f32[64,3]{0,1:T(4,128)} %param.14) | copy-start | bytes 2308
  0.0 7.6 %copy-start.3 = (f32[64]{0:T(128)S(1)}, f32[64]{0:T(128)}, u32[]{:S(2)}) copy-start(f32[64]{0:T(128)} %param.13) | copy-start | bytes 772
  0.0 7.6 %copy-start.2 = (f32[64]{0:T(128)S(1)}, f32[64]{0:T(128)}, u32[]{:S(2)}) copy-start(f32[64]{0:T(128)} %param.11) | copy-start | bytes 772
  3.6 6.8 %collective-permute-start = (bf16[80,128]{1,0:T(8,128)(2,1)S(1)}, bf16[80,128]{1,0:T(8,128)(2,1)S(1)}, u32[]{:S(2)}, u32[]{:S(2)}) collective-permute-start(bf16[80,128]{1,0:T(8,128)(2,1)S(1)} %get-tuple-element.28), channel_id=1, source_target_pairs={{0,1},{1,2},{2,3},{3,0},{4,5},{5,6},{6,7},{7,4},{8,9},{9,10},{10,1... | collective-permute-start | bytes 61448 | tf_op jit(solution)/shard_map/ppermute | solution.py:458
  6.6 3.8 %collective-permute-start.1 = (bf16[80,128]{1,0:T(8,128)(2,1)S(1)}, bf16[80,128]{1,0:T(8,128)(2,1)S(1)}, u32[]{:S(2)}, u32[]{:S(2)}) collective-permute-start(bf16[80,128]{1,0:T(8,128)(2,1)S(1)} %get-tuple-element.29), channel_id=1, source_target_pairs={{1,0},{2,1},{3,2},{0,3},{5,4},{6,5},{7,6},{4,7},{9,8},{10,9},{11,1... | collective-permute-start | bytes 61448 | tf_op jit(solution)/shard_map/ppermute | solution.py:459
  8.1 7.3 %collective-permute-start.2 = (f32[3,2,32]{2,1,0:T(2,128)S(1)}, f32[3,2,32]{2,1,0:T(2,128)S(1)}, u32[]{:S(2)}, u32[]{:S(2)}) collective-permute-start(f32[3,2,32]{2,1,0:T(2,128)S(1)} %get-tuple-element.32.refs_2_), channel_id=1, source_target_pairs={{0,2},{1,3},{2,0},{3,1},{4,6},{5,7},{6,4},{7,5},{8,10},{9,11},{10,... | collective-permute-start | bytes 2312 | tf_op jit(solution)/shard_map/ppermute | solution.py:478
  10.6 6.0 %collective-permute-start.3 = (bf16[256,128]{1,0:T(8,128)(2,1)S(1)}, bf16[256,128]{1,0:T(8,128)(2,1)S(1)}, u32[]{:S(2)}, u32[]{:S(2)}) collective-permute-start(bf16[256,128]{1,0:T(8,128)(2,1)S(1)} %get-tuple-element.35), channel_id=1, source_target_pairs={{4,8},{8,4},{12,16},{16,12},{20,24},{24,20},{28,0},{0,28},{5,9},{9... | collective-permute-start | bytes 196616 | tf_op jit(solution)/shard_map/ppermute | solution.py:426
  13.6 3.0 %collective-permute-start.4 = (bf16[256,128]{1,0:T(8,128)(2,1)S(1)}, bf16[256,128]{1,0:T(8,128)(2,1)S(1)}, u32[]{:S(2)}, u32[]{:S(2)}) collective-permute-start(bf16[256,128]{1,0:T(8,128)(2,1)S(1)} %get-tuple-element.36), channel_id=1, source_target_pairs={{0,4},{4,0},{8,12},{12,8},{16,20},{20,16},{24,28},{28,24},{1,5},{5... | collective-permute-start | bytes 196616 | tf_op jit(solution)/shard_map/ppermute | solution.py:426
  13.6 1.8 %copy-start = (bf16[64,64]{1,0:T(8,128)(2,1)S(1)}, bf16[64,64]{1,0:T(8,128)(2,1)}, u32[]{:S(2)}) copy-start(bf16[64,64]{1,0:T(8,128)(2,1)} %mix.3) | copy-start | bytes 24580

commit v4 on v2

--- a/solution.py
+++ b/solution.py
@@ -11,6 +11,7 @@
 ZOUT = 2
 CF = 16
 ROWS = 8
+GROUP = 4
 SPLIT = 1
 STORED = 32
 DW_BIAS, PW_BIAS, LIFT = 0, 1, 2
@@ -181,7 +182,9 @@
                         depth[z, out, to, :] = shifted_sum(*(sums.pop((out, dy)) for dy in (-1, 0, 1)))
 
 
-def outer_kernel(widths, weights, dw_bias, pw_bias, lift, coarse, cells_in, cells, extras, rims, own_block, stacked):
+def outer_kernel(
+    widths, weights, dw_bias, pw_bias, lift, mix, coarse, cells_in, cells, extras, rims, own_block, mixer, stacked
+):
     width = widths[lax.axis_index("gx")]
     channels, tile = weights.shape[1:]
     slots = cells.shape[1] // channels
@@ -204,6 +207,15 @@
                     ]
                     parts = [sum(weight * row for weight, row in zip(weights_of, rows)) for weights_of in tap]
                     rims[z, 2 * side + r, at, :] = shifted_sum(*parts)
+    wide = jnp.concatenate([mix[...]] * GROUP, axis=1)
+    wide = jnp.concatenate([wide] * GROUP, axis=0)
+    size = GROUP * channels
+    row, column = row_iota((size, size)), lane_iota((size, size))
+    same = sum(
+        ((row >= i * channels) & (row < (i + 1) * channels) & (column >= i * channels) & (column < (i + 1) * channels)).astype(F32)
+        for i in range(GROUP)
+    )
+    mixer[...] = jnp.where(same > 0, wide.astype(F32), 0.0).astype(BF16)
     for r in range(2):
 
         @pl.when(width + r < slots)
@@ -215,9 +227,9 @@
 def convolve_blocks(widths, cells, weights, depth, first, last):
     width = widths[lax.axis_index("gx")]
     slots = cells.shape[1] // weights.shape[1]
-    for limit in range(ROWS, slots + 1, ROWS):
-
-        @pl.when((width > limit - ROWS) & (width <= limit))
+    for limit in range(ROWS, slots + 1, GROUP):
+
+        @pl.when((width > limit - GROUP) & (width <= limit))
         def _():
             def convolve(b, carry):
                 convolve_block(cells, weights, depth, b, first, limit)
@@ -283,12 +295,12 @@
     return jnp.maximum(mixed, 0.2 * mixed)
 
 
-def mix_kernel(gathered, widths, mix, cells, extras, depth, rest, edge, *refs):
+def mix_kernel(gathered, widths, mixer, cells, extras, depth, rest, edge, *refs):
     if gathered:
-        coarse, value, ends, bases, lifted, across, mixer = refs
+        coarse, value, ends, bases, lifted, across = refs
         parts, ncx, ncy = coarse.shape
     else:
-        first, second, own_block, opposite, value, ends, bases, lifted, across, mixer, blocks = refs
+        first, second, own_block, opposite, value, ends, bases, lifted, across, blocks = refs
         parts, own_rows, ncy = own_block.shape
         ncx = 4 * own_rows
     width = widths[lax.axis_index("gx")]
@@ -323,16 +335,7 @@
             total = term if total is None else total + term
         lifted[i] = total
 
-    group = 4
-    wide = jnp.concatenate([mix[...]] * group, axis=1)
-    wide = jnp.concatenate([wide] * group, axis=0)
-    size = group * channels
-    row, column = row_iota((size, size)), lane_iota((size, size))
-    same = sum(
-        ((row >= i * channels) & (row < (i + 1) * channels) & (column >= i * channels) & (column < (i + 1) * channels)).astype(F32)
-        for i in range(group)
-    )
-    mixer[...] = jnp.where(same > 0, wide.astype(F32), 0.0).astype(BF16)
+    group = GROUP
 
     def mix_rows(begin, end):
         for x in range(begin, end, group):
@@ -345,7 +348,7 @@
                 for z in range(ZOUT):
                     part = mixed[i * channels : (i + 1) * channels, z * tile : (z + 1) * tile]
                     part = active(extras, part) + base_row(cells, lifted, phase, z, x + i)
-                    if x + i >= end - ROWS and begin:
+                    if x + i >= end - GROUP and begin:
                         part = jnp.where(x + i < width, part, 0.0)
                     value[z, pl.ds(x + i, channels, stride=slots), :] = part
 
@@ -361,8 +364,8 @@
             for z in range(ZOUT):
                 value[z, pl.ds(x, channels, stride=slots), :] = jnp.zeros((channels, tile), F32)
 
-    for limit in range(ROWS, slots + 1, ROWS):
-        pl.when((width > limit - ROWS) & (width <= limit))(lambda limit=limit: further_rows(limit))
+    for limit in range(ROWS, slots + 1, GROUP):
+        pl.when((width > limit - GROUP) & (width <= limit))(lambda limit=limit: further_rows(limit))
 
 
 def finish_kernel(widths, mix, extras, ends, bases, far, near, value_in, out, value, block, sems):
@@ -453,22 +456,24 @@
     )(pinned(feature), *(pinned(array) for array in small))
     first = lax.ppermute(first, "gy", [(i, (i + 1) % ny) for i in range(ny)])
     second = lax.ppermute(second, "gy", [((i + 1) % ny, i) for i in range(ny)])
-    cells, extras, rims, own_block = pl.pallas_call(
+    cells, extras, rims, own_block, mixer = pl.pallas_call(
         outer_kernel,
         out_shape=(
             cells_shape,
             pltpu.VMEM((5, channels, tile), F32),
             pltpu.VMEM((ZOUT, 4, channels, tile), F32),
             pltpu.VMEM(coarse.shape, F32),
+            pltpu.VMEM((GROUP * channels, GROUP * channels), BF16),
         ),
-        in_specs=[smem] + [vmem] * 6,
-        out_specs=(vmem,) * 4,
+        in_specs=[smem] + [vmem] * 7,
+        out_specs=(vmem,) * 5,
         scratch_shapes=[pltpu.VMEM((8, channels), F32)],
-        input_output_aliases={6: 0},
+        input_output_aliases={7: 0},
         compiler_params=params,
         cost_estimate=pl.CostEstimate(flops=10**8, bytes_accessed=10**6, transcendentals=0),
     )(
-        slab_widths, weights, dw_bias.reshape(1, channels), pw_bias.reshape(1, channels), lift_weight.T, block, cells
+        slab_widths, weights, dw_bias.reshape(1, channels), pw_bias.reshape(1, channels), lift_weight.T, pw_weight,
+        block, cells,
     )
     if not gathered:
         opposite = lax.ppermute(own_block, "gy", [(i, (i + 2) % 4) for i in range(4)])
@@ -508,12 +513,11 @@
         scratch_shapes=[
             pltpu.VMEM((3, channels, tile), F32),
             pltpu.VMEM((parts, ncx, tile), F32),
-            pltpu.VMEM((4 * channels, 4 * channels), BF16),
         ]
         + ([] if gathered else [pltpu.VMEM((parts, ncx, ncy), F32)]),
         compiler_params=params,
         cost_estimate=pl.CostEstimate(flops=10**9, bytes_accessed=10**6, transcendentals=0),
-    )(slab_widths, pw_weight, cells, extras, depth, rest, edge, *blocks)
+    )(slab_widths, mixer, cells, extras, depth, rest, edge, *blocks)
     out, _ = pl.pallas_call(
         finish_kernel,
         out_shape=(shape((ZOUT, channels, slots, tile), BF16), value_shape),

time: 16.9 us -> 17.3 us (1.024)
  the two profiles are of different devices: /device:TPU:0 before, /device:TPU:1 now
where the time goes in v4:
time: 17.3 us; the launch traced here: 17.2 us
  Pallas kernels  8.79 us (51%)
  starting transfers between devices  8.24 us (48%)
    ppermute x2, starting transfers between devices, swapped(): return lax.ppermute(array, axis, pairs)  3.69 us
    pallas_call x1, Pallas kernels, shards(): pl.pallas_call(pack_kernel, out_shape=(cells_shape, pltpu.VMEM((27, chann...  2.75 us
    pallas_call x1, Pallas kernels, shards(): pl.pallas_call(rest_kernel, out_shape=pltpu.VMEM((ZOUT, slots, channels -...  2.59 us
    ppermute x1, starting transfers between devices, shards(): first = lax.ppermute(first, 'gy', [(i, (i + 1) % ny) for i in range(ny)])  2.09 us
    ppermute x1, starting transfers between devices, shards(): lax.ppermute(own_block, 'gy', [(i, (i + 2) % 4) for i in range(4)])  1.44 us
    pallas_call x1, Pallas kernels, shards(): pl.pallas_call(functools.partial(mix_kernel, gathered), out_shape=(value_...  1.35 us
    pallas_call x1, Pallas kernels, shards(): pl.pallas_call(finish_kernel, out_shape=(shape((ZOUT, channels, slots, ti...  1.13 us
    ppermute x1, starting transfers between devices, shards(): second = lax.ppermute(second, 'gy', [((i + 1) % ny, i) for i in range(ny)])  1.02 us
  transfers between devices with their start and end apart: 5, of which 0 were waited for; matrix products, arithmetic and copies ran while one was open for 0% of the time, Pallas kernels for 29%

profile of v4, /device:TPU:1, one launch (start us, length us, event | category | flops | bytes accessed | tf_op | source)
XLA Modules:
  0.0 17.2 jit_solution(18437968326308842389)
XLA Ops:
  0.0 0.0 copy-start
  0.0 0.0 copy-start.1
  0.0 0.0 copy-start.3
  0.0 0.0 copy-start.2
  0.0 2.7 %shard_map.82 = (f32[6,1536,128]{2,1,0:T(8,128)S(1)}, f32[27,64,128]{2,1,0:T(8,128)S(1)}, bf16[80,128]{1,0:T(8,128)(2,1)S(1)}, bf16[80,128]{1,0:T(8,128)(2,1)S(1...) custom-call(bf16[6,64,24,128]{3,2,1,0:T(8,128)(2,1)} %feature.1, s32[8]{0:T(128)} %widths_in.1, f32[27,64]{1,0:T(8,128)} %taps_in.1, ...), custom_call_target="tpu_custom_call" | custom-call | tf_op jit(solution)/shard_map/pallas_call | solution.py:433
  2.8 2.1 %collective-permute-start = (bf16[80,128]{1,0:T(8,128)(2,1)S(1)}, bf16[80,128]{1,0:T(8,128)(2,1)S(1)}, u32[]{:S(2)}, u32[]{:S(2)}) collective-permute-start(bf16[80,128]{1,0:T(8,128)(2,1)S(1)} %get-tuple-element.30), channel_id=1, source_target_pairs={{0,1},{1,2},{2,3},{3,0},{4,5},{5,6},{6,7},{7,4},{8,9},{9,10},{10,1... | collective-permute-start | bytes 61448 | tf_op jit(solution)/shard_map/ppermute | solution.py:457
  4.9 1.0 %collective-permute-start.1 = (bf16[80,128]{1,0:T(8,128)(2,1)S(1)}, bf16[80,128]{1,0:T(8,128)(2,1)S(1)}, u32[]{:S(2)}, u32[]{:S(2)}) collective-permute-start(bf16[80,128]{1,0:T(8,128)(2,1)S(1)} %get-tuple-element.31), channel_id=1, source_target_pairs={{1,0},{2,1},{3,2},{0,3},{5,4},{6,5},{7,6},{4,7},{9,8},{10,9},{11,1... | collective-permute-start | bytes 61448 | tf_op jit(solution)/shard_map/ppermute | solution.py:458
  5.9 0.0 copy-done
  5.9 0.0 copy-done.1
  5.9 0.0 copy-done.3
  5.9 0.0 copy-done.2
  5.9 0.4 %shard_map.83 = (f32[6,1536,128]{2,1,0:T(8,128)S(1)}, f32[5,64,128]{2,1,0:T(8,128)S(1)}, f32[2,4,64,128]{3,2,1,0:T(8,128)S(1)}, f32[3,2,32]{2,1,0:T(2,128)S(1)}, bf16[256,256]{1,0:T(8,128)(2,1)S(1)}) custom-call(s32[8]{0:T(128)S(4)} %get-tuple-element.23.widths, f32[27,64,128]{2,1,0:T(8,128)S(1)} %get-tuple-element.24.weights, ...), custom_call_target="tpu_custom_call", output_to_operand_aliasing={{0}: (7, {})} | custom-call | flops 100000000 | bytes 1000000 | tf_op jit(solution)/shard_map/pallas_call | solution.py:459
  6.3 1.4 %collective-permute-start.2 = (f32[3,2,32]{2,1,0:T(2,128)S(1)}, f32[3,2,32]{2,1,0:T(2,128)S(1)}, u32[]{:S(2)}, u32[]{:S(2)}) collective-permute-start(f32[3,2,32]{2,1,0:T(2,128)S(1)} %get-tuple-element.34.refs_2_), channel_id=1, source_target_pairs={{0,2},{1,3},{2,0},{3,1},{4,6},{5,7},{6,4},{7,5},{8,10},{9,11},{10,... | collective-permute-start | bytes 2312 | tf_op jit(solution)/shard_map/ppermute | solution.py:479
  7.8 0.4 %shard_map.84.depth = f32[2,24,8,128]{3,2,1,0:T(8,128)S(1)} custom-call(s32[8]{0:T(128)S(4)} %get-tuple-element.23.widths, f32[6,1536,128]{2,1,0:T(8,128)S(1)} %get-tuple-element.29.cells, f32[27,64,128]{2,1,0:T(8,128)S(1)} %get-tuple-element.24.weights), custom_call_target="tpu_custom_call" | custom-call | flops 1000000000 | bytes 1000000 | tf_op jit(solution)/shard_map/pallas_call | solution.py:481
  8.1 0.0 collective-permute-done.first.refs_0_
  8.1 0.0 collective-permute-done.1.second.refs_1_
  8.2 0.2 %shard_map.85 = (f32[2,64,128]{2,1,0:T(8,128)S(1)}, bf16[256,128]{1,0:T(8,128)(2,1)S(1)}, bf16[256,128]{1,0:T(8,128)(2,1)S(1)}) custom-call(s32[8]{0:T(128)S(4)} %get-tuple-element.23.widths, bf16[80,128]{1,0:T(8,128)(2,1)S(1)} %collective-permute-done.first.refs_0_, bf16[80,128]{1,0:T(8,128)(2,1)S(1)} %collective-permute-done.1.second.refs_1_, ...), custom_call_target="tpu_custom_call" | custom-call | tf_op jit(solution)/shard_map/pallas_call | solution.py:489
  8.4 2.7 %collective-permute-start.3 = (bf16[256,128]{1,0:T(8,128)(2,1)S(1)}, bf16[256,128]{1,0:T(8,128)(2,1)S(1)}, u32[]{:S(2)}, u32[]{:S(2)}) collective-permute-start(bf16[256,128]{1,0:T(8,128)(2,1)S(1)} %get-tuple-element.37), channel_id=1, source_target_pairs={{4,8},{8,4},{12,16},{16,12},{20,24},{24,20},{28,0},{0,28},{5,9},{9... | collective-permute-start | bytes 196616 | tf_op jit(solution)/shard_map/ppermute | solution.py:425
  11.0 1.0 %collective-permute-start.4 = (bf16[256,128]{1,0:T(8,128)(2,1)S(1)}, bf16[256,128]{1,0:T(8,128)(2,1)S(1)}, u32[]{:S(2)}, u32[]{:S(2)}) collective-permute-start(bf16[256,128]{1,0:T(8,128)(2,1)S(1)} %get-tuple-element.38), channel_id=1, source_target_pairs={{0,4},{4,0},{8,12},{12,8},{16,20},{20,16},{24,28},{28,24},{1,5},{5... | collective-permute-start | bytes 196616 | tf_op jit(solution)/shard_map/ppermute | solution.py:425
  12.0 2.6 %shard_map.86.rest = f32[2,24,56,128]{3,2,1,0:T(8,128)S(1)} custom-call(s32[8]{0:T(128)S(4)} %get-tuple-element.23.widths, f32[2,64,128]{2,1,0:T(8,128)S(1)} %get-tuple-element.33.edge, f32[6,1536,128]{2,1,0:T(8,128)S(1)} %get-tuple-element.29.cells, f32[27,64,128]{2,1,0:T(8,128)S(1)} %get-tuple-element.24.weights), custom_call_target="tpu_custom_call" | custom-call | flops 1000000000 | bytes 1000000 | tf_op jit(solution)/shard_map/pallas_call | solution.py:499
  14.6 0.0 collective-permute-done.2.refs_3_
  14.7 1.3 %shard_map.87 = (f32[2,1536,128]{2,1,0:T(8,128)S(1)}, f32[2,4,64,128]{3,2,1,0:T(8,128)S(1)}, f32[2,4,64,128]{3,2,1,0:T(8,128)S(1)}) custom-call(s32[8]{0:T(128)S(4)} %get-tuple-element.23.widths, bf16[256,256]{1,0:T(8,128)(2,1)S(1)} %get-tuple-element.28.mixer, f32[6,1536,128]{2,1,0:T(8,128)S(1)} %get-tuple-element.29.cells, ...), custom_call_target="tpu_custom_call" | custom-call | flops 1000000000 | bytes 1000000 | tf_op jit(solution)/shard_map/pallas_call | solution.py:508
  16.0 0.0 collective-permute-done.3.far
  16.0 0.0 collective-permute-done.4.near
  16.0 1.1 %shard_map.88 = (bf16[2,64,24,128]{3,2,1,0:T(8,128)(2,1)}, f32[2,1536,128]{2,1,0:T(8,128)S(1)}) custom-call(s32[8]{0:T(128)S(4)} %get-tuple-element.23.widths, bf16[64,64]{1,0:T(8,128)(2,1)S(1)} %copy-done, f32[5,64,128]{2,1,0:T(8,128)S(1)} %get-tuple-element.27.extras, ...), custom_call_target="tpu_custom_call", output_to_operand_aliasing={{1}: (7, {})} | custom-call | tf_op jit(solution)/shard_map/pallas_call | solution.py:521
Async XLA Ops:
  0.0 5.9 %copy-start = (bf16[64,64]{1,0:T(8,128)(2,1)S(1)}, bf16[64,64]{1,0:T(8,128)(2,1)}, u32[]{:S(2)}) copy-start(bf16[64,64]{1,0:T(8,128)(2,1)} %mix.3) | copy-start | bytes 24580
  0.0 5.9 %copy-start.1 = (f32[64,3]{0,1:T(4,128)S(1)}, f32[64,3]{0,1:T(4,128)}, u32[]{:S(2)}) copy-start(f32[64,3]{0,1:T(4,128)} %param.14) | copy-start | bytes 2308
  0.0 5.9 %copy-start.3 = (f32[64]{0:T(128)S(1)}, f32[64]{0:T(128)}, u32[]{:S(2)}) copy-start(f32[64]{0:T(128)} %param.13) | copy-start | bytes 772
  0.0 5.9 %copy-start.2 = (f32[64]{0:T(128)S(1)}, f32[64]{0:T(128)}, u32[]{:S(2)}) copy-start(f32[64]{0:T(128)} %param.11) | copy-start | bytes 772
  2.8 5.4 %collective-permute-start = (bf16[80,128]{1,0:T(8,128)(2,1)S(1)}, bf16[80,128]{1,0:T(8,128)(2,1)S(1)}, u32[]{:S(2)}, u32[]{:S(2)}) collective-permute-start(bf16[80,128]{1,0:T(8,128)(2,1)S(1)} %get-tuple-element.30), channel_id=1, source_target_pairs={{0,1},{1,2},{2,3},{3,0},{4,5},{5,6},{6,7},{7,4},{8,9},{9,10},{10,1... | collective-permute-start | bytes 61448 | tf_op jit(solution)/shard_map/ppermute | solution.py:457
  4.9 3.3 %collective-permute-start.1 = (bf16[80,128]{1,0:T(8,128)(2,1)S(1)}, bf16[80,128]{1,0:T(8,128)(2,1)S(1)}, u32[]{:S(2)}, u32[]{:S(2)}) collective-permute-start(bf16[80,128]{1,0:T(8,128)(2,1)S(1)} %get-tuple-element.31), channel_id=1, source_target_pairs={{1,0},{2,1},{3,2},{0,3},{5,4},{6,5},{7,6},{4,7},{9,8},{10,9},{11,1... | collective-permute-start | bytes 61448 | tf_op jit(solution)/shard_map/ppermute | solution.py:458
  6.3 8.3 %collective-permute-start.2 = (f32[3,2,32]{2,1,0:T(2,128)S(1)}, f32[3,2,32]{2,1,0:T(2,128)S(1)}, u32[]{:S(2)}, u32[]{:S(2)}) collective-permute-start(f32[3,2,32]{2,1,0:T(2,128)S(1)} %get-tuple-element.34.refs_2_), channel_id=1, source_target_pairs={{0,2},{1,3},{2,0},{3,1},{4,6},{5,7},{6,4},{7,5},{8,10},{9,11},{10,... | collective-permute-start | bytes 2312 | tf_op jit(solution)/shard_map/ppermute | solution.py:479
  8.4 7.7 %collective-permute-start.3 = (bf16[256,128]{1,0:T(8,128)(2,1)S(1)}, bf16[256,128]{1,0:T(8,128)(2,1)S(1)}, u32[]{:S(2)}, u32[]{:S(2)}) collective-permute-start(bf16[256,128]{1,0:T(8,128)(2,1)S(1)} %get-tuple-element.37), channel_id=1, source_target_pairs={{4,8},{8,4},{12,16},{16,12},{20,24},{24,20},{28,0},{0,28},{5,9},{9... | collective-permute-start | bytes 196616 | tf_op jit(solution)/shard_map/ppermute | solution.py:425
  11.0 5.0 %collective-permute-start.4 = (bf16[256,128]{1,0:T(8,128)(2,1)S(1)}, bf16[256,128]{1,0:T(8,128)(2,1)S(1)}, u32[]{:S(2)}, u32[]{:S(2)}) collective-permute-start(bf16[256,128]{1,0:T(8,128)(2,1)S(1)} %get-tuple-element.38), channel_id=1, source_target_pairs={{0,4},{4,0},{8,12},{12,8},{16,20},{20,16},{24,28},{28,24},{1,5},{5... | collective-permute-start | bytes 196616 | tf_op jit(solution)/shard_map/ppermute | solution.py:425
